TPU v7x, 32 devices: a whole 2x2x4 slice. The times are simulated.
32 devices in a mesh: ens: 4 (over z), role: 2 (over core), gx: 4 (over y, x).
Axes of the slice: x: 2, y: 2, z: 4, core: 2. Of those that a mesh axis runs over, the one named last changes fastest.
Arguments:
- start_conc: float32 [4, 64, 256, 256], P('ens', 'gx', 'role'), may hold values from 0.1 to 4
- target: float32 [4, 64, 256, 256], P('ens', 'gx', 'role'), may hold values from -7 to 7
- log_coef: float32 [64, 256, 256], P('gx', 'role'), may hold values from -0.7 to 0
- inv_temp: float32 [64], replicated, may hold values from 1 to 1.06
- sched_start: int32 [4], P('ens'), may hold values from 0 to 60
Outputs:
- coef_grad: float32 [64, 256, 256], P('gx', 'role')
- adjoint_start: float32 [4, 64, 256, 256], P('ens', 'gx', 'role')
- final_conc: float32 [4, 64, 256, 256], P('ens', 'gx', 'role')
Inputs may be any that keep to these rules, and one draw needn't show every extreme that they name: `sched_start`: the plan entry at which each member's window begins.
All inputs are finite; a program needn't handle non-finite values.
Results may differ from a plain program's by a relative error of at most 0.00002.
Values sent between devices are 32-bit elements; how exact they have to be, the bound alone decides.
A program may use at most 128 MiB of HBM per device.

v0:
```python
import jax
import jax.numpy as jnp
from jax import lax
from jax.sharding import PartitionSpec as P

STEPS = 4


def extended(block, sides, width):
    for axis, dim in sides:
        count = lax.axis_size(axis)
        forward = [(i, i + 1) for i in range(count - 1)]
        backward = [(target, source) for source, target in forward]
        low = lax.ppermute(
            lax.slice_in_dim(block, block.shape[dim] - width, None, axis=dim), axis, forward
        )
        high = lax.ppermute(lax.slice_in_dim(block, 0, width, axis=dim), axis, backward)
        block = jnp.concatenate([low, block, high], axis=dim)
    return block


def neighbours(padded):
    padded = jnp.pad(padded, ((0, 0), (0, 0), (1, 1)))
    middle = padded[1:-1, 1:-1, 1:-1]
    near = [
        padded[2:, 1:-1, 1:-1],
        padded[:-2, 1:-1, 1:-1],
        padded[1:-1, 2:, 1:-1],
        padded[1:-1, :-2, 1:-1],
        padded[1:-1, 1:-1, 2:],
        padded[1:-1, 1:-1, :-2],
    ]
    return (middle, near)


def diffuse(field_ext, coef_ext):
    field_mid, field_near = neighbours(field_ext)
    coef_mid, coef_near = neighbours(coef_ext)
    result = jnp.zeros_like(field_mid)
    for field_nb, coef_nb in zip(field_near, coef_near):
        result = result + 0.5 * (coef_mid + coef_nb) * (field_nb - field_mid)
    return result


def sensitivity(adjoint_ext, conc_ext):
    adjoint_mid, adjoint_near = neighbours(adjoint_ext)
    conc_mid, conc_near = neighbours(conc_ext)
    result = jnp.zeros_like(conc_mid)
    for adjoint_nb, conc_nb in zip(adjoint_near, conc_near):
        result = result + (adjoint_mid - adjoint_nb) * (conc_mid - conc_nb)
    return -0.5 * result


def opening(coef, beginning, weights, depth_cells):
    coef_ext = extended(coef, (("role", 1), ("gx", 0)), depth_cells)
    state_ext = extended(beginning, (("role", 1), ("gx", 0)), depth_cells)
    target_ext = extended(weights, (("role", 1), ("gx", 0)), depth_cells)
    return (coef_ext, state_ext, target_ext)


def shards(start_conc, target, log_coef, inv_temp, sched_start):
    coef = jnp.exp(log_coef)
    beginning = start_conc[0]
    weights = target[0]
    inverse_temps = lax.dynamic_slice_in_dim(inv_temp, sched_start[0], STEPS)
    rate_list = 0.16 * jnp.exp(4.0 * (1.0 - inverse_temps))
    gradient = jnp.zeros(coef.shape, jnp.float32)
    coef_ext, padded, target_ext = opening(coef, beginning, weights, 1)
    current = beginning
    states = []
    for step in range(STEPS):
        if step > 0:
            padded = extended(current, (("role", 1), ("gx", 0)), 1)
        states.append(padded)
        current = current + rate_list[step] * diffuse(padded, coef_ext)
    adjoint = weights
    padded = target_ext
    for step in reversed(range(STEPS)):
        if step < STEPS - 1:
            padded = extended(adjoint, (("role", 1), ("gx", 0)), 1)
        gradient = gradient + rate_list[step] * sensitivity(padded, states[step])
        adjoint = adjoint + rate_list[step] * diffuse(padded, coef_ext)
    coef_grad = coef * lax.psum(gradient, "ens")
    return (coef_grad, adjoint[None], current[None])


def solution(mesh):
    placed = (
        P("ens", "gx", "role", None),
        P("ens", "gx", "role", None),
        P("gx", "role", None),
        P(),
        P("ens"),
    )
    return jax.shard_map(
        shards,
        mesh=mesh,
        in_specs=placed,
        out_specs=(
            P("gx", "role", None),
            P("ens", "gx", "role", None),
            P("ens", "gx", "role", None),
        ),
        check_vma=False,
    )
```

profile of v0, /device:TPU:6, one launch (start us, length us, event | category | flops | bytes accessed | tf_op | source)
XLA Modules:
  0.0 333.3 jit_solution(4834817663286200408)
XLA Ops:
  7.2 1.0 fusion.218
  8.2 1.7 collective-permute-start
  10.0 1.3 collective-permute-start.1
  11.3 1.0 fusion.217
  12.3 3.0 collective-permute-start.6
  15.3 1.3 collective-permute-start.7
  16.6 1.9 exp.6
  18.5 1.3 collective-permute-start.4
  21.2 3.0 collective-permute-start.3
  24.3 1.0 pad_maximum_fusion.96
  25.3 1.3 collective-permute-start.10
  26.6 4.7 %collective-permute-start.8 = (f32[1,130,256]{2,1,0:T(8,128)S(1)}, f32[1,130,256]{2,1,0:T(8,128)S(1)}, u32[]{:S(2)}, u32[]{:S(2)}) collective-permute-start(f32[1,130,256]{2,1,0:T(8,128)S(1)} %get-tuple-element.20), channel_id=1, source_target_pairs={{1,0},{2,1},{3,2},{5,4},{6,5},{7,6},{9,8},{10,9},{11,10},{13,12},{... | collective-permute-start | bytes 399368 | tf_op jit(solution)/shard_map/ppermute | solution.py:17
  31.3 1.3 collective-permute-start.22
  32.7 4.6 %collective-permute-start.2 = (f32[1,130,256]{2,1,0:T(8,128)S(1)}, f32[1,130,256]{2,1,0:T(8,128)S(1)}, u32[]{:S(2)}, u32[]{:S(2)}) collective-permute-start(f32[1,130,256]{2,1,0:T(8,128)S(1)} %get-tuple-element.22), channel_id=1, source_target_pairs={{1,0},{2,1},{3,2},{5,4},{6,5},{7,6},{9,8},{10,9},{11,10},{13,12},{... | collective-permute-start | bytes 399368 | tf_op jit(solution)/shard_map/ppermute | solution.py:17
  37.3 4.2 %collective-permute-start.5 = (f32[1,130,256]{2,1,0:T(8,128)S(1)}, f32[1,130,256]{2,1,0:T(8,128)S(1)}, u32[]{:S(2)}, u32[]{:S(2)}) collective-permute-start(f32[1,130,256]{2,1,0:T(8,128)S(1)} %get-tuple-element.19), channel_id=1, source_target_pairs={{1,0},{2,1},{3,2},{5,4},{6,5},{7,6},{9,8},{10,9},{11,10},{13,12},{... | collective-permute-start | bytes 399368 | tf_op jit(solution)/shard_map/ppermute | solution.py:17
  41.5 1.3 collective-permute-start.9
  42.9 4.4 %select_maximum_fusion.28 = f32[18,130,258]{2,1,0:T(8,128)} fusion(f32[1,130,256]{2,1,0:T(8,128)S(1)} %collective-permute-done.8, f32[1,130,256]{2,1,0:T(8,128)S(1)} %collective-permute-done.10, f32[16,1,256]{2,1,0:T(1,128)S(1)} %collective-permute-done.7, f32[16,128,256]{2,1,0:T(8,128)S(1)} %bitcast.17, f32[16,1,256]{2,1,0:T(1,128)S(1)} %collective-permute-done.6), kind=kLoop, calls=%fused_computation.30 | loop fusion | flops 7244640 | bytes 4811040 | tf_op jit(solution)/shard_map/concatenate | solution.py:18
  47.2 1.3 collective-permute-done.9
  48.5 4.4 %select_maximum_fusion.32 = f32[18,130,258]{2,1,0:T(8,128)} fusion(f32[1,130,256]{2,1,0:T(8,128)S(1)} %collective-permute-done.5, f32[1,130,256]{2,1,0:T(8,128)S(1)} %collective-permute-done.9, f32[16,1,256]{2,1,0:T(1,128)S(1)} %collective-permute-done.4, f32[16,128,256]{2,1,0:T(8,128)S(1)} %exp.6, f32[16,1,256]{2,1,0:T(1,128)S(1)} %collective-permute-done.3), kind=kLoop, calls=%fused_computation.34 | loop fusion | flops 7244640 | bytes 4811040 | tf_op jit(solution)/shard_map/concatenate | solution.py:18
  52.9 3.1 select_maximum_fusion.16
  56.0 10.0 %fusion.185 = (f32[16,128,256]{2,1,0:T(8,128)S(1)}, f32[16,128,256]{2,1,0:T(8,128)S(1)}, f32[16,128,256]{2,1,0:T(8,128)S(1)}) fusion(f32[16,128,256]{2,1,0:T(8,128)S(1)} %bitcast.18, f32[16,1,256]{2,1,0:T(1,128)S(1)} %collective-permute-done.6, f32[16,1,256]{2,1,0:T(1,128)S(1)} %collective-permute-done.7, f32[1,130,256]{2,1,0:T(8,128)} %copy-done.26, ...), kind=kLoop, calls=%fused_computation.279 | loop fusion | flops 24641536 | bytes 21569540 | tf_op jit(solution)/shard_map/add | solution.py:75
  66.0 9.7 %fusion.113 = f32[16,128,256]{2,1,0:T(8,128)S(1)} fusion(f32[16,128,256]{2,1,0:T(8,128)} %bitcast.20, f32[16,1,256]{2,1,0:T(1,128)S(1)} %collective-permute-done, f32[16,1,256]{2,1,0:T(1,128)S(1)} %collective-permute-done.1, f32[1,130,256]{2,1,0:T(8,128)} %copy-done.30, f32[1,130,256]{2,1,0:T(8,128)} %copy-done.32, ...), kind=kLoop, calls=%fused_computation.177 | loop fusion | flops 22544384 | bytes 15278084 | tf_op jit(solution)/shard_map/add | solution.py:82
  75.8 1.3 collective-permute-start.24
  77.1 1.3 collective-permute-start.25
  78.4 3.0 collective-permute-start.11
  81.5 1.3 collective-permute-start.12
  82.8 1.3 collective-permute-start.27
  84.1 4.6 %collective-permute-start.26 = (f32[1,130,256]{2,1,0:T(8,128)S(1)}, f32[1,130,256]{2,1,0:T(8,128)S(1)}, u32[]{:S(2)}, u32[]{:S(2)}) collective-permute-start(f32[1,130,256]{2,1,0:T(8,128)S(1)} %get-tuple-element.16), channel_id=1, source_target_pairs={{1,0},{2,1},{3,2},{5,4},{6,5},{7,6},{9,8},{10,9},{11,10},{13,12},{... | collective-permute-start | bytes 399368 | tf_op jit(solution)/shard_map/ppermute | solution.py:17
  88.8 1.3 collective-permute-start.14
  90.1 5.0 %collective-permute-start.13 = (f32[1,130,256]{2,1,0:T(8,128)S(1)}, f32[1,130,256]{2,1,0:T(8,128)S(1)}, u32[]{:S(2)}, u32[]{:S(2)}) collective-permute-start(f32[1,130,256]{2,1,0:T(8,128)S(1)} %get-tuple-element.10), channel_id=1, source_target_pairs={{1,0},{2,1},{3,2},{5,4},{6,5},{7,6},{9,8},{10,9},{11,10},{13,12},{... | collective-permute-start | bytes 399368 | tf_op jit(solution)/shard_map/ppermute | solution.py:17
  95.2 3.1 select_maximum_fusion.8
  98.3 5.5 %fusion.69 = f32[16,128,256]{2,1,0:T(8,128)S(1)} fusion(f32[16,128,256]{2,1,0:T(8,128)S(1)} %fusion.113, f32[16,1,256]{2,1,0:T(1,128)S(1)} %collective-permute-done.24, f32[16,1,256]{2,1,0:T(1,128)S(1)} %collective-permute-done.25, f32[1,130,256]{2,1,0:T(8,128)S(1)} %collective-permute-done.27, f32[1,130,256]{2,1,0:T(8,128)S(1)} %collective-permute-done.26, ...), kind=kLoop, calls=%fused_computation.124 | loop fusion | flops 22544384 | bytes 15278084 | tf_op jit(solution)/shard_map/add | solution.py:82
  103.8 2.2 collective-permute-start.28
  106.0 1.3 collective-permute-start.29
  107.4 3.1 select_maximum_fusion.24
  110.5 5.5 %fusion.164 = f32[16,128,256]{2,1,0:T(8,128)S(1)} fusion(f32[16,128,256]{2,1,0:T(8,128)S(1)} %get-tuple-element.3, f32[16,1,256]{2,1,0:T(1,128)S(1)} %collective-permute-done.11, f32[16,1,256]{2,1,0:T(1,128)S(1)} %collective-permute-done.12, f32[1,130,256]{2,1,0:T(8,128)S(1)} %collective-permute-done.14, f32[1,130,256]{2,1,0:T(8,128)S(1)} %collective-permute-done.13, ...), kind=kLoop, calls=%fused_computation.248 | loop fusion | flops 22544384 | bytes 15278084 | tf_op jit(solution)/shard_map/add | solution.py:75
  116.1 3.0 collective-permute-start.15
  119.1 1.3 collective-permute-start.16
  120.5 1.3 collective-permute-start.31
  121.8 5.2 %collective-permute-start.30 = (f32[1,130,256]{2,1,0:T(8,128)S(1)}, f32[1,130,256]{2,1,0:T(8,128)S(1)}, u32[]{:S(2)}, u32[]{:S(2)}) collective-permute-start(f32[1,130,256]{2,1,0:T(8,128)S(1)} %get-tuple-element.14), channel_id=1, source_target_pairs={{1,0},{2,1},{3,2},{5,4},{6,5},{7,6},{9,8},{10,9},{11,10},{13,12},{... | collective-permute-start | bytes 399368 | tf_op jit(solution)/shard_map/ppermute | solution.py:17
  127.1 1.3 collective-permute-start.18
  128.4 5.4 %collective-permute-start.17 = (f32[1,130,256]{2,1,0:T(8,128)S(1)}, f32[1,130,256]{2,1,0:T(8,128)S(1)}, u32[]{:S(2)}, u32[]{:S(2)}) collective-permute-start(f32[1,130,256]{2,1,0:T(8,128)S(1)} %get-tuple-element.8), channel_id=1, source_target_pairs={{1,0},{2,1},{3,2},{5,4},{6,5},{7,6},{9,8},{10,9},{11,10},{13,12},{... | collective-permute-start | bytes 399368 | tf_op jit(solution)/shard_map/ppermute | solution.py:17
  133.9 3.1 select_maximum_fusion.4
  137.0 5.5 %fusion.39 = f32[16,128,256]{2,1,0:T(8,128)S(1)} fusion(f32[16,128,256]{2,1,0:T(8,128)S(1)} %fusion.69, f32[16,1,256]{2,1,0:T(1,128)S(1)} %collective-permute-done.28, f32[16,1,256]{2,1,0:T(1,128)S(1)} %collective-permute-done.29, f32[1,130,256]{2,1,0:T(8,128)S(1)} %collective-permute-done.31, f32[1,130,256]{2,1,0:T(8,128)S(1)} %collective-permute-done.30, ...), kind=kLoop, calls=%fused_computation.86 | loop fusion | flops 22544384 | bytes 15278084 | tf_op jit(solution)/shard_map/add | solution.py:82
  142.6 2.2 collective-permute-start.32
  144.8 1.3 collective-permute-start.33
  146.2 3.1 select_maximum_fusion.20
  149.3 5.5 %fusion.145 = f32[16,128,256]{2,1,0:T(8,128)S(1)} fusion(f32[16,128,256]{2,1,0:T(8,128)S(1)} %fusion.164, f32[16,1,256]{2,1,0:T(1,128)S(1)} %collective-permute-done.15, f32[16,1,256]{2,1,0:T(1,128)S(1)} %collective-permute-done.16, f32[1,130,256]{2,1,0:T(8,128)S(1)} %collective-permute-done.18, f32[1,130,256]{2,1,0:T(8,128)S(1)} %collective-permute-done.17, ...), kind=kLoop, calls=%fused_computation.221 | loop fusion | flops 22544384 | bytes 15278084 | tf_op jit(solution)/shard_map/add | solution.py:75
  154.9 3.0 collective-permute-start.19
  157.9 1.3 collective-permute-start.20
  159.3 1.3 collective-permute-start.35
  160.6 5.2 %collective-permute-start.34 = (f32[1,130,256]{2,1,0:T(8,128)S(1)}, f32[1,130,256]{2,1,0:T(8,128)S(1)}, u32[]{:S(2)}, u32[]{:S(2)}) collective-permute-start(f32[1,130,256]{2,1,0:T(8,128)S(1)} %get-tuple-element.12), channel_id=1, source_target_pairs={{1,0},{2,1},{3,2},{5,4},{6,5},{7,6},{9,8},{10,9},{11,10},{13,12},{... | collective-permute-start | bytes 399368 | tf_op jit(solution)/shard_map/ppermute | solution.py:17
  168.3 1.1 pad_maximum_fusion.85
  169.4 1.3 collective-permute-start.23
  170.7 5.8 %collective-permute-start.21 = (f32[1,130,256]{2,1,0:T(8,128)S(1)}, f32[1,130,256]{2,1,0:T(8,128)S(1)}, u32[]{:S(2)}, u32[]{:S(2)}) collective-permute-start(f32[1,130,256]{2,1,0:T(8,128)S(1)} %get-tuple-element.6), channel_id=1, source_target_pairs={{1,0},{2,1},{3,2},{5,4},{6,5},{7,6},{9,8},{10,9},{11,10},{13,12},{... | collective-permute-start | bytes 399368 | tf_op jit(solution)/shard_map/ppermute | solution.py:17
  176.6 4.3 %select_maximum_fusion = f32[18,130,258]{2,1,0:T(8,128)} fusion(f32[1,130,256]{2,1,0:T(8,128)S(1)} %collective-permute-done.34, f32[1,130,256]{2,1,0:T(8,128)S(1)} %collective-permute-done.35, f32[16,1,256]{2,1,0:T(1,128)S(1)} %collective-permute-done.33, f32[16,128,256]{2,1,0:T(8,128)S(1)} %copy-done.13, f32[16,1,256]{2,1,0:T(1,128)S(1)} %collective-permute-done.32), kind=kLoop, calls=%fused_computation.2 | loop fusion | flops 7244640 | bytes 4811040 | tf_op jit(solution)/shard_map/concatenate | solution.py:18
  182.4 3.8 %select_maximum_fusion.12 = f32[18,130,258]{2,1,0:T(8,128)S(1)} fusion(f32[1,130,256]{2,1,0:T(8,128)S(1)} %collective-permute-done.21, f32[1,130,256]{2,1,0:T(8,128)S(1)} %collective-permute-done.23, f32[16,1,256]{2,1,0:T(1,128)} %copy-done.62, f32[16,128,256]{2,1,0:T(8,128)S(1)} %copy-done.15, f32[16,1,256]{2,1,0:T(1,128)} %copy-done.60), kind=kLoop, calls=%fused_computation.14 | loop fusion | flops 7244640 | bytes 4811040 | tf_op jit(solution)/shard_map/concatenate | solution.py:18
  186.3 1.9 copy-done.22
  188.3 45.0 %fusion.15 = f32[16,128,256]{2,1,0:T(8,128)} fusion(f32[16,128,256]{2,1,0:T(8,128)S(1)} %copy-done.13, f32[16,1,256]{2,1,0:T(1,128)} %copy-done.56, f32[16,1,256]{2,1,0:T(1,128)} %copy-done.58, f32[1,130,256]{2,1,0:T(8,128)} %copy-done.42, f32[1,130,256]{2,1,0:T(8,128)} %copy-done.44, f32[16,128,256]{2,1,0:T(8,128)S(1)} %copy-done.9, ...), kind=kLoop, calls=%fused_computation.54 | loop fusion | flops 85458944 | bytes 54820880 | tf_op jit(solution)/shard_map/add | solution.py:81
  233.3 0.8 copy-done.43
  234.3 13.3 %fusion.9 = f32[1,16,128,256]{3,2,1,0:T(8,128)} fusion(f32[16,128,256]{2,1,0:T(8,128)} %copy-done.12, f32[16,1,256]{2,1,0:T(1,128)S(1)} %copy-done.57, f32[16,1,256]{2,1,0:T(1,128)S(1)} %copy-done.59, f32[1,130,256]{2,1,0:T(8,128)S(1)} %copy-done.43, f32[1,130,256]{2,1,0:T(8,128)S(1)} %copy-done.45, f32[16,128,256]{2,1,0:T(8,128)} %copy-done.2, ...), kind=kLoop, calls=%fused_computation.48 | loop fusion | flops 22544384 | bytes 15278084 | tf_op jit(solution)/shard_map/broadcast_in_dim | solution.py:84
  247.7 6.4 %fusion.100 = f32[1,16,128,256]{3,2,1,0:T(8,128)} fusion(f32[16,128,256]{2,1,0:T(8,128)S(1)} %copy-done.16, f32[16,1,256]{2,1,0:T(1,128)S(1)} %copy-done.61, f32[16,1,256]{2,1,0:T(1,128)S(1)} %copy-done.63, f32[1,130,256]{2,1,0:T(8,128)S(1)} %copy-done.47, f32[1,130,256]{2,1,0:T(8,128)S(1)} %copy-done.49, f32[16,128,256]{2,1,0:T(8,128)S(1)} %copy-done.3, ...), kind=kLoop, calls=%fused_computation.163 | loop fusion | flops 22544384 | bytes 15278084 | tf_op jit(solution)/shard_map/broadcast_in_dim | solution.py:84
  254.1 68.5 %all-reduce.11.cloned.1.call-done = f32[16,128,256]{2,1,0:T(8,128)} async-done(((f32[16,128,256]{2,1,0:T(8,128)}), f32[16,128,256]{2,1,0:T(8,128)}) %all-reduce.11.cloned.1.call-update) | async-done | bytes 2097168 | tf_op jit(solution)/shard_map/psum | solution.py:83
  322.6 3.8 %exponential_multiply_fusion.1 = f32[16,128,256]{2,1,0:T(8,128)} fusion(f32[16,128,256]{2,1,0:T(8,128)} %all-reduce.11.cloned.1.call-done, f32[16,128,256]{2,1,0:T(8,128)} %param.7), kind=kLoop, calls=%fused_computation.348 | loop fusion | flops 524288 | bytes 6291456 | tf_op jit(solution)/shard_map/mul | solution.py:83
  (181 shorter events, 2.9 us)
Async XLA Ops:
  7.2 315.5 %all-reduce.11.cloned.1.call-start = ((), (), s32[]{:S(2)}) async-start(), calls=%async_computation | async-start | bytes 4194304 | tf_op jit(solution)/shard_map/psum | solution.py:83
  8.2 18.4 %collective-permute-start = (f32[16,1,256]{2,1,0:T(1,128)S(1)}, f32[16,1,256]{2,1,0:T(1,128)S(1)}, u32[]{:S(2)}, u32[]{:S(2)}) collective-permute-start(f32[16,1,256]{2,1,0:T(1,128)S(1)} %get-tuple-element.41), channel_id=1, source_target_pairs={{0,4},{1,5},{2,6},{3,7},{8,12},{9,13},{10,14},{11,15},{16,20},{17,... | collective-permute-start | bytes 49160 | tf_op jit(solution)/shard_map/ppermute | solution.py:14
  10.0 21.3 %collective-permute-start.1 = (f32[16,1,256]{2,1,0:T(1,128)S(1)}, f32[16,1,256]{2,1,0:T(1,128)S(1)}, u32[]{:S(2)}, u32[]{:S(2)}) collective-permute-start(f32[16,1,256]{2,1,0:T(1,128)S(1)} %get-tuple-element.40), channel_id=1, source_target_pairs={{4,0},{5,1},{6,2},{7,3},{12,8},{13,9},{14,10},{15,11},{20,16},{21,... | collective-permute-start | bytes 49160 | tf_op jit(solution)/shard_map/ppermute | solution.py:17
  12.3 9.0 %collective-permute-start.6 = (f32[16,1,256]{2,1,0:T(1,128)S(1)}, f32[16,1,256]{2,1,0:T(1,128)S(1)}, u32[]{:S(2)}, u32[]{:S(2)}) collective-permute-start(f32[16,1,256]{2,1,0:T(1,128)S(1)} %get-tuple-element.39), channel_id=1, source_target_pairs={{0,4},{1,5},{2,6},{3,7},{8,12},{9,13},{10,14},{11,15},{16,20},{17,... | collective-permute-start | bytes 49160 | tf_op jit(solution)/shard_map/ppermute | solution.py:14
  15.3 9.0 %collective-permute-start.7 = (f32[16,1,256]{2,1,0:T(1,128)S(1)}, f32[16,1,256]{2,1,0:T(1,128)S(1)}, u32[]{:S(2)}, u32[]{:S(2)}) collective-permute-start(f32[16,1,256]{2,1,0:T(1,128)S(1)} %get-tuple-element.38), channel_id=1, source_target_pairs={{4,0},{5,1},{6,2},{7,3},{12,8},{13,9},{14,10},{15,11},{20,16},{21,... | collective-permute-start | bytes 49160 | tf_op jit(solution)/shard_map/ppermute | solution.py:17
  18.5 14.1 %collective-permute-start.4 = (f32[16,1,256]{2,1,0:T(1,128)S(1)}, f32[16,1,256]{2,1,0:T(1,128)S(1)}, u32[]{:S(2)}, u32[]{:S(2)}) collective-permute-start(f32[16,1,256]{2,1,0:T(1,128)S(1)} %get-tuple-element.37), channel_id=1, source_target_pairs={{4,0},{5,1},{6,2},{7,3},{12,8},{13,9},{14,10},{15,11},{20,16},{21,... | collective-permute-start | bytes 49160 | tf_op jit(solution)/shard_map/ppermute | solution.py:17
  21.2 16.0 %collective-permute-start.3 = (f32[16,1,256]{2,1,0:T(1,128)S(1)}, f32[16,1,256]{2,1,0:T(1,128)S(1)}, u32[]{:S(2)}, u32[]{:S(2)}) collective-permute-start(f32[16,1,256]{2,1,0:T(1,128)S(1)} %get-tuple-element.36), channel_id=1, source_target_pairs={{0,4},{1,5},{2,6},{3,7},{8,12},{9,13},{10,14},{11,15},{16,20},{17,... | collective-permute-start | bytes 49160 | tf_op jit(solution)/shard_map/ppermute | solution.py:14
  25.3 16.2 %collective-permute-start.10 = (f32[1,130,256]{2,1,0:T(8,128)S(1)}, f32[1,130,256]{2,1,0:T(8,128)S(1)}, u32[]{:S(2)}, u32[]{:S(2)}) collective-permute-start(f32[1,130,256]{2,1,0:T(8,128)S(1)} %get-tuple-element.21), channel_id=1, source_target_pairs={{0,1},{1,2},{2,3},{4,5},{5,6},{6,7},{8,9},{9,10},{10,11},{12,13},{... | collective-permute-start | bytes 399368 | tf_op jit(solution)/shard_map/ppermute | solution.py:14
  26.6 16.3 %copy-start.24 = (f32[1,16,128,256]{3,2,1,0:T(8,128)S(1)}, f32[1,16,128,256]{3,2,1,0:T(8,128)}, u32[]{:S(2)}) copy-start(f32[1,16,128,256]{3,2,1,0:T(8,128)} %param.5) | copy-start | bytes 6291460
  26.6 16.2 %collective-permute-start.8 = (f32[1,130,256]{2,1,0:T(8,128)S(1)}, f32[1,130,256]{2,1,0:T(8,128)S(1)}, u32[]{:S(2)}, u32[]{:S(2)}) collective-permute-start(f32[1,130,256]{2,1,0:T(8,128)S(1)} %get-tuple-element.20), channel_id=1, source_target_pairs={{1,0},{2,1},{3,2},{5,4},{6,5},{7,6},{9,8},{10,9},{11,10},{13,12},{... | collective-permute-start | bytes 399368 | tf_op jit(solution)/shard_map/ppermute | solution.py:17
  31.3 21.5 %collective-permute-start.22 = (f32[1,130,256]{2,1,0:T(8,128)S(1)}, f32[1,130,256]{2,1,0:T(8,128)S(1)}, u32[]{:S(2)}, u32[]{:S(2)}) collective-permute-start(f32[1,130,256]{2,1,0:T(8,128)S(1)} %get-tuple-element.23), channel_id=1, source_target_pairs={{0,1},{1,2},{2,3},{4,5},{5,6},{6,7},{8,9},{9,10},{10,11},{12,13},{... | collective-permute-start | bytes 399368 | tf_op jit(solution)/shard_map/ppermute | solution.py:14
  32.7 20.2 %collective-permute-start.2 = (f32[1,130,256]{2,1,0:T(8,128)S(1)}, f32[1,130,256]{2,1,0:T(8,128)S(1)}, u32[]{:S(2)}, u32[]{:S(2)}) collective-permute-start(f32[1,130,256]{2,1,0:T(8,128)S(1)} %get-tuple-element.22), channel_id=1, source_target_pairs={{1,0},{2,1},{3,2},{5,4},{6,5},{7,6},{9,8},{10,9},{11,10},{13,12},{... | collective-permute-start | bytes 399368 | tf_op jit(solution)/shard_map/ppermute | solution.py:17
  37.3 10.0 %collective-permute-start.5 = (f32[1,130,256]{2,1,0:T(8,128)S(1)}, f32[1,130,256]{2,1,0:T(8,128)S(1)}, u32[]{:S(2)}, u32[]{:S(2)}) collective-permute-start(f32[1,130,256]{2,1,0:T(8,128)S(1)} %get-tuple-element.19), channel_id=1, source_target_pairs={{1,0},{2,1},{3,2},{5,4},{6,5},{7,6},{9,8},{10,9},{11,10},{13,12},{... | collective-permute-start | bytes 399368 | tf_op jit(solution)/shard_map/ppermute | solution.py:17
  41.5 6.9 %collective-permute-start.9 = (f32[1,130,256]{2,1,0:T(8,128)S(1)}, f32[1,130,256]{2,1,0:T(8,128)S(1)}, u32[]{:S(2)}, u32[]{:S(2)}) collective-permute-start(f32[1,130,256]{2,1,0:T(8,128)S(1)} %get-tuple-element.18), channel_id=1, source_target_pairs={{0,1},{1,2},{2,3},{4,5},{5,6},{6,7},{8,9},{9,10},{10,11},{12,13},{... | collective-permute-start | bytes 399368 | tf_op jit(solution)/shard_map/ppermute | solution.py:14
  66.0 44.5 %copy-start.4 = (f32[16,128,256]{2,1,0:T(8,128)}, f32[16,128,256]{2,1,0:T(8,128)S(1)}, u32[]{:S(2)}) copy-start(f32[16,128,256]{2,1,0:T(8,128)S(1)} %get-tuple-element.3) | copy-start | bytes 6291460
  66.0 83.3 %copy-start = (f32[16,128,256]{2,1,0:T(8,128)}, f32[16,128,256]{2,1,0:T(8,128)S(1)}, u32[]{:S(2)}) copy-start(f32[16,128,256]{2,1,0:T(8,128)S(1)} %get-tuple-element.4) | copy-start | bytes 6291460
  66.0 83.3 %copy-start.2 = (f32[16,128,256]{2,1,0:T(8,128)}, f32[16,128,256]{2,1,0:T(8,128)S(1)}, u32[]{:S(2)}) copy-start(f32[16,128,256]{2,1,0:T(8,128)S(1)} %get-tuple-element.5) | copy-start | bytes 6291460
  75.8 22.5 %copy-start.6 = (f32[16,128,256]{2,1,0:T(8,128)}, f32[16,128,256]{2,1,0:T(8,128)S(1)}, u32[]{:S(2)}) copy-start(f32[16,128,256]{2,1,0:T(8,128)S(1)} %fusion.113) | copy-start | bytes 6291460
  75.8 7.0 %collective-permute-start.24 = (f32[16,1,256]{2,1,0:T(1,128)S(1)}, f32[16,1,256]{2,1,0:T(1,128)S(1)}, u32[]{:S(2)}, u32[]{:S(2)}) collective-permute-start(f32[16,1,256]{2,1,0:T(1,128)S(1)} %get-tuple-element.35), channel_id=1, source_target_pairs={{0,4},{1,5},{2,6},{3,7},{8,12},{9,13},{10,14},{11,15},{16,20},{17,... | collective-permute-start | bytes 49160 | tf_op jit(solution)/shard_map/ppermute | solution.py:14
  77.1 5.7 %collective-permute-start.25 = (f32[16,1,256]{2,1,0:T(1,128)S(1)}, f32[16,1,256]{2,1,0:T(1,128)S(1)}, u32[]{:S(2)}, u32[]{:S(2)}) collective-permute-start(f32[16,1,256]{2,1,0:T(1,128)S(1)} %get-tuple-element.34), channel_id=1, source_target_pairs={{4,0},{5,1},{6,2},{7,3},{12,8},{13,9},{14,10},{15,11},{20,16},{21,... | collective-permute-start | bytes 49160 | tf_op jit(solution)/shard_map/ppermute | solution.py:17
  78.4 10.3 %collective-permute-start.11 = (f32[16,1,256]{2,1,0:T(1,128)S(1)}, f32[16,1,256]{2,1,0:T(1,128)S(1)}, u32[]{:S(2)}, u32[]{:S(2)}) collective-permute-start(f32[16,1,256]{2,1,0:T(1,128)S(1)} %get-tuple-element.29), channel_id=1, source_target_pairs={{0,4},{1,5},{2,6},{3,7},{8,12},{9,13},{10,14},{11,15},{16,20},{17,... | collective-permute-start | bytes 49160 | tf_op jit(solution)/shard_map/ppermute | solution.py:14
  81.5 7.2 %collective-permute-start.12 = (f32[16,1,256]{2,1,0:T(1,128)S(1)}, f32[16,1,256]{2,1,0:T(1,128)S(1)}, u32[]{:S(2)}, u32[]{:S(2)}) collective-permute-start(f32[16,1,256]{2,1,0:T(1,128)S(1)} %get-tuple-element.28), channel_id=1, source_target_pairs={{4,0},{5,1},{6,2},{7,3},{12,8},{13,9},{14,10},{15,11},{20,16},{21,... | collective-permute-start | bytes 49160 | tf_op jit(solution)/shard_map/ppermute | solution.py:17
  82.8 12.3 %collective-permute-start.27 = (f32[1,130,256]{2,1,0:T(8,128)S(1)}, f32[1,130,256]{2,1,0:T(8,128)S(1)}, u32[]{:S(2)}, u32[]{:S(2)}) collective-permute-start(f32[1,130,256]{2,1,0:T(8,128)S(1)} %get-tuple-element.17), channel_id=1, source_target_pairs={{0,1},{1,2},{2,3},{4,5},{5,6},{6,7},{8,9},{9,10},{10,11},{12,13},{... | collective-permute-start | bytes 399368 | tf_op jit(solution)/shard_map/ppermute | solution.py:14
  84.1 11.0 %collective-permute-start.26 = (f32[1,130,256]{2,1,0:T(8,128)S(1)}, f32[1,130,256]{2,1,0:T(8,128)S(1)}, u32[]{:S(2)}, u32[]{:S(2)}) collective-permute-start(f32[1,130,256]{2,1,0:T(8,128)S(1)} %get-tuple-element.16), channel_id=1, source_target_pairs={{1,0},{2,1},{3,2},{5,4},{6,5},{7,6},{9,8},{10,9},{11,10},{13,12},{... | collective-permute-start | bytes 399368 | tf_op jit(solution)/shard_map/ppermute | solution.py:17
  88.7 21.8 %copy-start.50 = (f32[16,1,256]{2,1,0:T(1,128)}, f32[16,1,256]{2,1,0:T(1,128)S(1)}, u32[]{:S(2)}) copy-start(f32[16,1,256]{2,1,0:T(1,128)S(1)} %collective-permute-done.11) | copy-start | bytes 49156
  88.7 21.8 %copy-start.51 = (f32[16,1,256]{2,1,0:T(1,128)}, f32[16,1,256]{2,1,0:T(1,128)S(1)}, u32[]{:S(2)}) copy-start(f32[16,1,256]{2,1,0:T(1,128)S(1)} %collective-permute-done.12) | copy-start | bytes 49156
  88.8 18.5 %collective-permute-start.14 = (f32[1,130,256]{2,1,0:T(8,128)S(1)}, f32[1,130,256]{2,1,0:T(8,128)S(1)}, u32[]{:S(2)}, u32[]{:S(2)}) collective-permute-start(f32[1,130,256]{2,1,0:T(8,128)S(1)} %get-tuple-element.11), channel_id=1, source_target_pairs={{0,1},{1,2},{2,3},{4,5},{5,6},{6,7},{8,9},{9,10},{10,11},{12,13},{... | collective-permute-start | bytes 399368 | tf_op jit(solution)/shard_map/ppermute | solution.py:14
  90.1 17.3 %collective-permute-start.13 = (f32[1,130,256]{2,1,0:T(8,128)S(1)}, f32[1,130,256]{2,1,0:T(8,128)S(1)}, u32[]{:S(2)}, u32[]{:S(2)}) collective-permute-start(f32[1,130,256]{2,1,0:T(8,128)S(1)} %get-tuple-element.10), channel_id=1, source_target_pairs={{1,0},{2,1},{3,2},{5,4},{6,5},{7,6},{9,8},{10,9},{11,10},{13,12},{... | collective-permute-start | bytes 399368 | tf_op jit(solution)/shard_map/ppermute | solution.py:17
  103.8 33.2 %copy-start.8 = (f32[16,128,256]{2,1,0:T(8,128)}, f32[16,128,256]{2,1,0:T(8,128)S(1)}, u32[]{:S(2)}) copy-start(f32[16,128,256]{2,1,0:T(8,128)S(1)} %fusion.69) | copy-start | bytes 6291460
  103.8 16.6 %collective-permute-start.28 = (f32[16,1,256]{2,1,0:T(1,128)S(1)}, f32[16,1,256]{2,1,0:T(1,128)S(1)}, u32[]{:S(2)}, u32[]{:S(2)}) collective-permute-start(f32[16,1,256]{2,1,0:T(1,128)S(1)} %get-tuple-element.33), channel_id=1, source_target_pairs={{0,4},{1,5},{2,6},{3,7},{8,12},{9,13},{10,14},{11,15},{16,20},{17,... | collective-permute-start | bytes 49160 | tf_op jit(solution)/shard_map/ppermute | solution.py:14
  106.0 14.4 %collective-permute-start.29 = (f32[16,1,256]{2,1,0:T(1,128)S(1)}, f32[16,1,256]{2,1,0:T(1,128)S(1)}, u32[]{:S(2)}, u32[]{:S(2)}) collective-permute-start(f32[16,1,256]{2,1,0:T(1,128)S(1)} %get-tuple-element.32), channel_id=1, source_target_pairs={{4,0},{5,1},{6,2},{7,3},{12,8},{13,9},{14,10},{15,11},{20,16},{21,... | collective-permute-start | bytes 49160 | tf_op jit(solution)/shard_map/ppermute | solution.py:17
  116.1 33.2 %copy-start.10 = (f32[16,128,256]{2,1,0:T(8,128)}, f32[16,128,256]{2,1,0:T(8,128)S(1)}, u32[]{:S(2)}) copy-start(f32[16,128,256]{2,1,0:T(8,128)S(1)} %fusion.164) | copy-start | bytes 6291460
  116.1 10.9 %collective-permute-start.15 = (f32[16,1,256]{2,1,0:T(1,128)S(1)}, f32[16,1,256]{2,1,0:T(1,128)S(1)}, u32[]{:S(2)}, u32[]{:S(2)}) collective-permute-start(f32[16,1,256]{2,1,0:T(1,128)S(1)} %get-tuple-element.27), channel_id=1, source_target_pairs={{0,4},{1,5},{2,6},{3,7},{8,12},{9,13},{10,14},{11,15},{16,20},{17,... | collective-permute-start | bytes 49160 | tf_op jit(solution)/shard_map/ppermute | solution.py:14
  119.1 7.9 %collective-permute-start.16 = (f32[16,1,256]{2,1,0:T(1,128)S(1)}, f32[16,1,256]{2,1,0:T(1,128)S(1)}, u32[]{:S(2)}, u32[]{:S(2)}) collective-permute-start(f32[16,1,256]{2,1,0:T(1,128)S(1)} %get-tuple-element.26), channel_id=1, source_target_pairs={{4,0},{5,1},{6,2},{7,3},{12,8},{13,9},{14,10},{15,11},{20,16},{21,... | collective-permute-start | bytes 49160 | tf_op jit(solution)/shard_map/ppermute | solution.py:17
  120.4 16.5 %copy-start.52 = (f32[16,1,256]{2,1,0:T(1,128)}, f32[16,1,256]{2,1,0:T(1,128)S(1)}, u32[]{:S(2)}) copy-start(f32[16,1,256]{2,1,0:T(1,128)S(1)} %collective-permute-done.28) | copy-start | bytes 49156
  120.5 16.5 %copy-start.53 = (f32[16,1,256]{2,1,0:T(1,128)}, f32[16,1,256]{2,1,0:T(1,128)S(1)}, u32[]{:S(2)}) copy-start(f32[16,1,256]{2,1,0:T(1,128)S(1)} %collective-permute-done.29) | copy-start | bytes 49156
  120.5 13.3 %collective-permute-start.31 = (f32[1,130,256]{2,1,0:T(8,128)S(1)}, f32[1,130,256]{2,1,0:T(8,128)S(1)}, u32[]{:S(2)}, u32[]{:S(2)}) collective-permute-start(f32[1,130,256]{2,1,0:T(8,128)S(1)} %get-tuple-element.15), channel_id=1, source_target_pairs={{0,1},{1,2},{2,3},{4,5},{5,6},{6,7},{8,9},{9,10},{10,11},{12,13},{... | collective-permute-start | bytes 399368 | tf_op jit(solution)/shard_map/ppermute | solution.py:14
  121.8 12.0 %collective-permute-start.30 = (f32[1,130,256]{2,1,0:T(8,128)S(1)}, f32[1,130,256]{2,1,0:T(8,128)S(1)}, u32[]{:S(2)}, u32[]{:S(2)}) collective-permute-start(f32[1,130,256]{2,1,0:T(8,128)S(1)} %get-tuple-element.14), channel_id=1, source_target_pairs={{1,0},{2,1},{3,2},{5,4},{6,5},{7,6},{9,8},{10,9},{11,10},{13,12},{... | collective-permute-start | bytes 399368 | tf_op jit(solution)/shard_map/ppermute | solution.py:17
  127.0 22.3 %copy-start.54 = (f32[16,1,256]{2,1,0:T(1,128)}, f32[16,1,256]{2,1,0:T(1,128)S(1)}, u32[]{:S(2)}) copy-start(f32[16,1,256]{2,1,0:T(1,128)S(1)} %collective-permute-done.15) | copy-start | bytes 49156
  127.0 22.3 %copy-start.55 = (f32[16,1,256]{2,1,0:T(1,128)}, f32[16,1,256]{2,1,0:T(1,128)S(1)}, u32[]{:S(2)}) copy-start(f32[16,1,256]{2,1,0:T(1,128)S(1)} %collective-permute-done.16) | copy-start | bytes 49156
  127.1 19.0 %collective-permute-start.18 = (f32[1,130,256]{2,1,0:T(8,128)S(1)}, f32[1,130,256]{2,1,0:T(8,128)S(1)}, u32[]{:S(2)}, u32[]{:S(2)}) collective-permute-start(f32[1,130,256]{2,1,0:T(8,128)S(1)} %get-tuple-element.9), channel_id=1, source_target_pairs={{0,1},{1,2},{2,3},{4,5},{5,6},{6,7},{8,9},{9,10},{10,11},{12,13},{... | collective-permute-start | bytes 399368 | tf_op jit(solution)/shard_map/ppermute | solution.py:14
  128.4 17.8 %collective-permute-start.17 = (f32[1,130,256]{2,1,0:T(8,128)S(1)}, f32[1,130,256]{2,1,0:T(8,128)S(1)}, u32[]{:S(2)}, u32[]{:S(2)}) collective-permute-start(f32[1,130,256]{2,1,0:T(8,128)S(1)} %get-tuple-element.8), channel_id=1, source_target_pairs={{1,0},{2,1},{3,2},{5,4},{6,5},{7,6},{9,8},{10,9},{11,10},{13,12},{... | collective-permute-start | bytes 399368 | tf_op jit(solution)/shard_map/ppermute | solution.py:17
  142.6 16.7 %copy-start.12 = (f32[16,128,256]{2,1,0:T(8,128)}, f32[16,128,256]{2,1,0:T(8,128)S(1)}, u32[]{:S(2)}) copy-start(f32[16,128,256]{2,1,0:T(8,128)S(1)} %fusion.39) | copy-start | bytes 6291460
  142.6 16.6 %collective-permute-start.32 = (f32[16,1,256]{2,1,0:T(1,128)S(1)}, f32[16,1,256]{2,1,0:T(1,128)S(1)}, u32[]{:S(2)}, u32[]{:S(2)}) collective-permute-start(f32[16,1,256]{2,1,0:T(1,128)S(1)} %get-tuple-element.31), channel_id=1, source_target_pairs={{0,4},{1,5},{2,6},{3,7},{8,12},{9,13},{10,14},{11,15},{16,20},{17,... | collective-permute-start | bytes 49160 | tf_op jit(solution)/shard_map/ppermute | solution.py:14
  144.8 14.4 %collective-permute-start.33 = (f32[16,1,256]{2,1,0:T(1,128)S(1)}, f32[16,1,256]{2,1,0:T(1,128)S(1)}, u32[]{:S(2)}, u32[]{:S(2)}) collective-permute-start(f32[16,1,256]{2,1,0:T(1,128)S(1)} %get-tuple-element.30), channel_id=1, source_target_pairs={{4,0},{5,1},{6,2},{7,3},{12,8},{13,9},{14,10},{15,11},{20,16},{21,... | collective-permute-start | bytes 49160 | tf_op jit(solution)/shard_map/ppermute | solution.py:17
  154.9 13.4 %collective-permute-start.19 = (f32[16,1,256]{2,1,0:T(1,128)S(1)}, f32[16,1,256]{2,1,0:T(1,128)S(1)}, u32[]{:S(2)}, u32[]{:S(2)}) collective-permute-start(f32[16,1,256]{2,1,0:T(1,128)S(1)} %get-tuple-element.25), channel_id=1, source_target_pairs={{0,4},{1,5},{2,6},{3,7},{8,12},{9,13},{10,14},{11,15},{16,20},{17,... | collective-permute-start | bytes 49160 | tf_op jit(solution)/shard_map/ppermute | solution.py:14
  157.9 10.4 %collective-permute-start.20 = (f32[16,1,256]{2,1,0:T(1,128)S(1)}, f32[16,1,256]{2,1,0:T(1,128)S(1)}, u32[]{:S(2)}, u32[]{:S(2)}) collective-permute-start(f32[16,1,256]{2,1,0:T(1,128)S(1)} %get-tuple-element.24), channel_id=1, source_target_pairs={{4,0},{5,1},{6,2},{7,3},{12,8},{13,9},{14,10},{15,11},{20,16},{21,... | collective-permute-start | bytes 49160 | tf_op jit(solution)/shard_map/ppermute | solution.py:17
  159.2 17.4 %copy-start.56 = (f32[16,1,256]{2,1,0:T(1,128)}, f32[16,1,256]{2,1,0:T(1,128)S(1)}, u32[]{:S(2)}) copy-start(f32[16,1,256]{2,1,0:T(1,128)S(1)} %collective-permute-done.32) | copy-start | bytes 49156
  159.2 17.4 %copy-start.58 = (f32[16,1,256]{2,1,0:T(1,128)}, f32[16,1,256]{2,1,0:T(1,128)S(1)}, u32[]{:S(2)}) copy-start(f32[16,1,256]{2,1,0:T(1,128)S(1)} %collective-permute-done.33) | copy-start | bytes 49156
  159.3 17.3 %collective-permute-start.35 = (f32[1,130,256]{2,1,0:T(8,128)S(1)}, f32[1,130,256]{2,1,0:T(8,128)S(1)}, u32[]{:S(2)}, u32[]{:S(2)}) collective-permute-start(f32[1,130,256]{2,1,0:T(8,128)S(1)} %get-tuple-element.13), channel_id=1, source_target_pairs={{0,1},{1,2},{2,3},{4,5},{5,6},{6,7},{8,9},{9,10},{10,11},{12,13},{... | collective-permute-start | bytes 399368 | tf_op jit(solution)/shard_map/ppermute | solution.py:14
  160.6 16.0 %collective-permute-start.34 = (f32[1,130,256]{2,1,0:T(8,128)S(1)}, f32[1,130,256]{2,1,0:T(8,128)S(1)}, u32[]{:S(2)}, u32[]{:S(2)}) collective-permute-start(f32[1,130,256]{2,1,0:T(8,128)S(1)} %get-tuple-element.12), channel_id=1, source_target_pairs={{1,0},{2,1},{3,2},{5,4},{6,5},{7,6},{9,8},{10,9},{11,10},{13,12},{... | collective-permute-start | bytes 399368 | tf_op jit(solution)/shard_map/ppermute | solution.py:17
  168.3 12.7 %copy-start.60 = (f32[16,1,256]{2,1,0:T(1,128)}, f32[16,1,256]{2,1,0:T(1,128)S(1)}, u32[]{:S(2)}) copy-start(f32[16,1,256]{2,1,0:T(1,128)S(1)} %collective-permute-done.19) | copy-start | bytes 49156
  168.3 12.7 %copy-start.62 = (f32[16,1,256]{2,1,0:T(1,128)}, f32[16,1,256]{2,1,0:T(1,128)S(1)}, u32[]{:S(2)}) copy-start(f32[16,1,256]{2,1,0:T(1,128)S(1)} %collective-permute-done.20) | copy-start | bytes 49156
  169.4 11.6 %collective-permute-start.23 = (f32[1,130,256]{2,1,0:T(8,128)S(1)}, f32[1,130,256]{2,1,0:T(8,128)S(1)}, u32[]{:S(2)}, u32[]{:S(2)}) collective-permute-start(f32[1,130,256]{2,1,0:T(8,128)S(1)} %get-tuple-element.7), channel_id=1, source_target_pairs={{0,1},{1,2},{2,3},{4,5},{5,6},{6,7},{8,9},{9,10},{10,11},{12,13},{... | collective-permute-start | bytes 399368 | tf_op jit(solution)/shard_map/ppermute | solution.py:14
  170.7 11.7 %copy-start.15 = (f32[16,128,256]{2,1,0:T(8,128)S(1)}, f32[16,128,256]{2,1,0:T(8,128)}, u32[]{:S(2)}) copy-start(f32[16,128,256]{2,1,0:T(8,128)} %copy-done.14) | copy-start | bytes 6291460
  170.7 10.3 %collective-permute-start.21 = (f32[1,130,256]{2,1,0:T(8,128)S(1)}, f32[1,130,256]{2,1,0:T(8,128)S(1)}, u32[]{:S(2)}, u32[]{:S(2)}) collective-permute-start(f32[1,130,256]{2,1,0:T(8,128)S(1)} %get-tuple-element.6), channel_id=1, source_target_pairs={{1,0},{2,1},{3,2},{5,4},{6,5},{7,6},{9,8},{10,9},{11,10},{13,12},{... | collective-permute-start | bytes 399368 | tf_op jit(solution)/shard_map/ppermute | solution.py:17
  234.2 13.4 %copy-start.1 = (f32[16,128,256]{2,1,0:T(8,128)S(1)}, f32[16,128,256]{2,1,0:T(8,128)}, u32[]{:S(2)}) copy-start(f32[16,128,256]{2,1,0:T(8,128)} %copy-done) | copy-start | bytes 6291460
  234.2 13.4 %copy-start.3 = (f32[16,128,256]{2,1,0:T(8,128)S(1)}, f32[16,128,256]{2,1,0:T(8,128)}, u32[]{:S(2)}) copy-start(f32[16,128,256]{2,1,0:T(8,128)} %copy-done.2) | copy-start | bytes 6291460
  234.2 13.4 %copy-start.16 = (f32[16,128,256]{2,1,0:T(8,128)S(1)}, f32[16,128,256]{2,1,0:T(8,128)}, u32[]{:S(2)}) copy-start(f32[16,128,256]{2,1,0:T(8,128)} %copy-done.14) | copy-start | bytes 6291460
  234.2 13.4 %copy-start.23 = (f32[18,130,258]{2,1,0:T(8,128)S(1)}, f32[18,130,258]{2,1,0:T(8,128)}, u32[]{:S(2)}) copy-start(f32[18,130,258]{2,1,0:T(8,128)} %copy-done.22) | copy-start | bytes 7244644
  234.3 13.4 %copy-start.47 = (f32[1,130,256]{2,1,0:T(8,128)S(1)}, f32[1,130,256]{2,1,0:T(8,128)}, u32[]{:S(2)}) copy-start(f32[1,130,256]{2,1,0:T(8,128)} %copy-done.46) | copy-start | bytes 399364
  234.3 13.4 %copy-start.49 = (f32[1,130,256]{2,1,0:T(8,128)S(1)}, f32[1,130,256]{2,1,0:T(8,128)}, u32[]{:S(2)}) copy-start(f32[1,130,256]{2,1,0:T(8,128)} %copy-done.48) | copy-start | bytes 399364
  234.3 13.4 %copy-start.61 = (f32[16,1,256]{2,1,0:T(1,128)S(1)}, f32[16,1,256]{2,1,0:T(1,128)}, u32[]{:S(2)}) copy-start(f32[16,1,256]{2,1,0:T(1,128)} %copy-done.60) | copy-start | bytes 49156
  234.3 13.4 %copy-start.63 = (f32[16,1,256]{2,1,0:T(1,128)S(1)}, f32[16,1,256]{2,1,0:T(1,128)}, u32[]{:S(2)}) copy-start(f32[16,1,256]{2,1,0:T(1,128)} %copy-done.62) | copy-start | bytes 49156
  (38 other events, 184.9 us)
Sparse Core Ops, SparseCore 0:
  233.4 89.1 all-reduce.10
where the time goes:
time: 336 us; the launch traced here: 333 us
  other arithmetic  145 us (43%)
  starting transfers between devices  90.5 us (27%)
  waiting for transfers between devices  69.9 us (21%)
  between operations  18.8 us (6%)
  local copies, waits for them, and re-layouts  9.16 us (3%)
    psum x1, waiting for transfers between devices, shards(): coef_grad = coef * lax.psum(gradient, 'ens')  68.5 us
    ppermute x18, starting transfers between devices, extended(): lax.ppermute(lax.slice_in_dim(block, 0, width, axis=dim), axis, backward)  56.3 us
    add x1, other arithmetic, shards(): gradient = gradient + rate_list[step] * sensitivity(padded, states[step])  45 us
    ppermute x18, starting transfers between devices, extended(): lax.ppermute(lax.slice_in_dim(block, block.shape[dim] - width, None, axis...  34.2 us
    concatenate x10, other arithmetic, extended(): block = jnp.concatenate([low, block, high], axis=dim)  32.4 us
    add x3, other arithmetic, shards(): current = current + rate_list[step] * diffuse(padded, coef_ext)  21 us
    add x3, other arithmetic, shards(): adjoint = adjoint + rate_list[step] * diffuse(padded, coef_ext)  20.7 us
    broadcast_in_dim x2, other arithmetic, shards(): return (coef_grad, adjoint[None], current[None])  19.7 us
  transfers between devices with their start and end apart: 37, of which 2 were waited for; matrix products, arithmetic and copies ran while one was open for 22% of the time, Pallas kernels for 0%

commit v1 on v0

v1 whole, which is shorter than its diff:
```python
import functools
import jax
import jax.numpy as jnp
from jax import lax
from jax.experimental import pallas as pl
from jax.experimental.pallas import tpu as pltpu
from jax.sharding import PartitionSpec as P

STEPS = 4
COEF = 2 * STEPS
ROWS = 32
FAR = -1e30


def body(
    sizes, rates, start, target, logc, grad_out, adj_out, conc_out,
    F, wx, wyp, wym, wz, D, G, E, M,
    load_sem, xs, xr, rs, rr, sa, sb, re, rm,
):
    ngx, nrole = sizes
    nx, ny, nz = logc.shape
    gx, role, ens = lax.axis_index("gx"), lax.axis_index("role"), lax.axis_index("ens")
    main = pl.ds(8, ny)
    lane = lax.broadcasted_iota(jnp.int32, (ROWS, nz), 1)
    first, last = lane == 0, lane == nz - 1
    chunks = range(8, 8 + ny, ROWS)
    is_end = jnp.logical_or(ens == 0, ens == 3)
    is_mid = jnp.logical_and(ens > 0, ens < 3)
    inputs = {0: start.at[0], STEPS: target.at[0], COEF: logc}
    axes = (("gx", gx, ngx), ("role", role, nrole))
    lower = [index > 0 for _, index, _ in axes]
    upper = [index < count - 1 for _, index, count in axes]

    def has_to(axis, d):
        return upper[axis] if d else lower[axis]

    def has_from(axis, d):
        return lower[axis] if d else upper[axis]

    def xcopy(f, d):
        own = nx if d else 1
        src = inputs[f].at[own - 1] if f in inputs else F.at[f, own, main]
        return pltpu.make_async_remote_copy(
            src, F.at[f, 0 if d else nx + 1, main], xs.at[2 * f + d], xr.at[2 * f + d],
            device_id={"gx": gx + (1 if d else -1)}, device_id_type=pl.DeviceIdType.MESH)

    def rcopy(f, d, part, lo, hi):
        planes = pl.ds(lo, hi - lo)
        row = ny - 8 if d else 0
        if f in inputs:
            src = inputs[f].at[:, pl.ds(row, 8)]
        else:
            src = F.at[f, planes, pl.ds(row + 8, 8)]
        sem = (2 * f + d) * 3 + part
        return pltpu.make_async_remote_copy(
            src, F.at[f, planes, pl.ds(0 if d else ny + 8, 8)], rs.at[sem], rr.at[sem],
            device_id={"role": role + (1 if d else -1)}, device_id_type=pl.DeviceIdType.MESH)

    def each(axis, make, do):
        for d in (0, 1):
            cond = has_from(axis, d) if do == "wait_recv" else has_to(axis, d)

            @pl.when(cond)
            def _():
                getattr(make(d), do)()

    def xdo(f, do):
        each(0, lambda d: xcopy(f, d), do)

    def rdo(f, part, lo, hi, do):
        each(1, lambda d: rcopy(f, d, part, lo, hi), do)

    barrier = pltpu.get_barrier_semaphore()
    total = jnp.int32(0)
    for name, index, count in axes + (("ens", ens, 4),):
        for cond, to in ((index > 0, -1), (index < count - 1, 1)):
            total = total + cond.astype(jnp.int32)

            @pl.when(cond)
            def _():
                pl.semaphore_signal(barrier, 1, device_id={name: index + to},
                                    device_id_type=pl.DeviceIdType.MESH)
    loads = [
        pltpu.make_async_copy(inputs[f], F.at[f, pl.ds(1, nx), main], load_sem.at[i])
        for i, f in enumerate((COEF, 0, STEPS))
    ]
    for load in loads:
        load.start()
    pl.semaphore_wait(barrier, total)

    for f in (COEF, 0, STEPS):
        rdo(f, 0, 1, nx + 1, "start")
    for f in (COEF, 0, STEPS):
        xdo(f, "start")

    for side in (0, 1):
        @pl.when(jnp.logical_not(upper[0] if side else lower[0]))
        def _():
            @pl.loop(0, COEF)
            def _(f):
                F[f, (nx + 1) * side, main, :] = jnp.zeros((ny, nz), jnp.float32)
            F[COEF, (nx + 1) * side, main, :] = jnp.full((ny, nz), FAR, jnp.float32)

        @pl.when(jnp.logical_not(upper[1] if side else lower[1]))
        def _():
            edge = pl.ds((ny + 8) * side, 8)

            @pl.loop(0, COEF)
            def _(f):
                F[f, pl.ds(1, nx), edge, :] = jnp.zeros((nx, 8, nz), jnp.float32)
            F[COEF, pl.ds(1, nx), edge, :] = jnp.full((nx, 8, nz), FAR, jnp.float32)

    loads[0].wait()
    rdo(COEF, 0, 1, nx + 1, "wait_recv")

    @pl.loop(1, nx + 1)
    def _(p):
        F[COEF, p] = 0.5 * jnp.exp(F[COEF, p])

    def wx_plane(p):
        wx[p] = F[COEF, p, main, :] + F[COEF, p + 1, main, :]

    def diag_plane(p):
        D[p - 1] = D[p - 1] + (wx[p - 1] + wx[p])

    @pl.loop(1, nx + 1)
    def _(p):
        for y in chunks:
            rows = pl.ds(y - 8, ROWS)
            k = F[COEF, p, pl.ds(y, ROWS), :]
            up = k + F[COEF, p, pl.ds(y + 1, ROWS), :]
            down = k + F[COEF, p, pl.ds(y - 1, ROWS), :]
            right = jnp.where(last, 0.0, k + pltpu.roll(k, nz - 1, 1))
            wyp[p - 1, rows, :] = up
            wym[p - 1, rows, :] = down
            wz[p - 1, rows, :] = right
            D[p - 1, rows, :] = (
                up + down + right + pltpu.roll(right, 1, 1)
                + jnp.where(jnp.logical_or(first, last), k, 0.0))

    pl.loop(1, nx)(wx_plane)
    pl.loop(2, nx)(diag_plane)

    def diffuse(k, lo, hi):
        pairs = ((k, rates[k]), (STEPS + k, rates[STEPS - 1 - k]))

        @pl.loop(lo, hi)
        def _(p):
            for y in chunks:
                rows, here = pl.ds(y - 8, ROWS), pl.ds(y, ROWS)
                w0, w1 = wx[p - 1, rows, :], wx[p, rows, :]
                wp, wm = wyp[p - 1, rows, :], wym[p - 1, rows, :]
                wr, diag = wz[p - 1, rows, :], D[p - 1, rows, :]
                for n, (f, rate) in enumerate(pairs):
                    v = F[f, p, here, :]
                    acc = w0 * F[f, p - 1, here, :] + w1 * F[f, p + 1, here, :]
                    acc = acc + wp * F[f, p, pl.ds(y + 1, ROWS), :]
                    acc = acc + wm * F[f, p, pl.ds(y - 1, ROWS), :]
                    acc = acc + wr * pltpu.roll(v, nz - 1, 1) + pltpu.roll(wr * v, 1, 1)
                    new = v + rate * (acc - diag * v)
                    if k < STEPS - 1:
                        F[f + 1, p, here, :] = new
                    elif n == 0:
                        conc_out[0, p - 1, rows, :] = new
                    else:
                        adj_out[0, p - 1, rows, :] = new

    def sens(p):
        for y in chunks:
            here = pl.ds(y, ROWS)
            up, down = pl.ds(y + 1, ROWS), pl.ds(y - 1, ROWS)
            result = None
            for s in range(STEPS):
                cf, af = s, STEPS + (STEPS - 1 - s)
                c, a = F[cf, p, here, :], F[af, p, here, :]
                acc = (a - F[af, p - 1, here, :]) * (c - F[cf, p - 1, here, :])
                acc = acc + (a - F[af, p + 1, here, :]) * (c - F[cf, p + 1, here, :])
                acc = acc + (a - F[af, p, up, :]) * (c - F[cf, p, up, :])
                acc = acc + (a - F[af, p, down, :]) * (c - F[cf, p, down, :])
                face = (a - jnp.where(last, 0.0, pltpu.roll(a, nz - 1, 1))) * (
                    c - jnp.where(last, 0.0, pltpu.roll(c, nz - 1, 1)))
                acc = acc + face + jnp.where(first, a * c, pltpu.roll(face, 1, 1))
                term = (-0.5 * rates[s]) * acc
                result = term if result is None else result + term
            G[p - 1, pl.ds(y - 8, ROWS), :] = result

    def ens_copy(src, dst, send, recv, to):
        return pltpu.make_async_remote_copy(
            src, dst, send, recv, device_id={"ens": to}, device_id_type=pl.DeviceIdType.MESH)

    quarter = nx // 4

    def plane(i):
        return lax.rem(i + quarter, nx)

    def end_send(i):
        q = plane(i)
        return ens_copy(G.at[q], E.at[q], sa.at[i], re.at[i], 1 + ens // 3)

    def peer_send(i):
        q = plane(i)
        return ens_copy(E.at[q], M.at[q], sa.at[i], rm.at[i], 3 - ens)

    def back_send(i):
        q = plane(i)
        return ens_copy(G.at[q], M.at[q], sb.at[i], rm.at[i], (ens - 1) * 3)

    def gradient(lo, hi):
        @pl.loop(lo, hi)
        def _(i):
            sens(plane(i) + 1)

            @pl.when(is_end)
            def _():
                end_send(i).start()

    def merge(lo, hi):
        @pl.when(is_mid)
        def _():
            @pl.loop(lo, hi)
            def _(i):
                q = plane(i)
                end_send(i).wait_recv()
                E[q] = E[q] + G[q]
                peer_send(i).start()

    def close(lo, hi):
        @pl.when(is_mid)
        def _():
            @pl.loop(lo, hi)
            def _(i):
                q = plane(i)
                peer_send(i).wait_recv()
                G[q] = E[q] + M[q]
                back_send(i).start()
                grad_out[q] = 2.0 * F[COEF, q + 1, main, :] * G[q]

    def finish(lo, hi):
        @pl.when(is_end)
        def _():
            @pl.loop(lo, hi)
            def _(i):
                q = plane(i)
                back_send(i).wait_recv()
                grad_out[q] = 2.0 * F[COEF, q + 1, main, :] * M[q]

    loads[1].wait()
    loads[2].wait()
    for f in (0, STEPS):
        rdo(f, 0, 1, nx + 1, "wait_recv")
    for k in range(STEPS - 1):
        lo, hi = k + 2, nx - k
        diffuse(k, lo, hi)
        for f in (k + 1, STEPS + k + 1):
            rdo(f, 0, lo, hi, "start")
        if k == 0:
            xdo(COEF, "wait_recv")
            for p in (0, nx + 1):
                F[COEF, p, main, :] = 0.5 * jnp.exp(F[COEF, p, main, :])
            wx_plane(0)
            wx_plane(nx)
            diag_plane(1)
            diag_plane(nx)
        for f in (k + 1, STEPS + k + 1):
            rdo(f, 0, lo, hi, "wait_recv")
    gradient(0, nx // 2)

    half = nx // 2
    third = half // 3
    for k in range(STEPS):
        for f in (k, STEPS + k):
            xdo(f, "wait_recv")
            if k > 0:
                rdo(f, 1, 1, k + 1, "wait_recv")
                rdo(f, 2, nx + 1 - k, nx + 1, "wait_recv")
        if k < STEPS - 1:
            diffuse(k, 1, k + 2)
            diffuse(k, nx - k, nx + 1)
            for f in (k + 1, STEPS + k + 1):
                xdo(f, "start")
                rdo(f, 1, 1, k + 2, "start")
                rdo(f, 2, nx - k, nx + 1, "start")
            if k == 0:
                merge(0, half // 2)
                diffuse(STEPS - 1, quarter + 1, nx - quarter + 1)
            elif k == 1:
                merge(half // 2, half)
                close(0, half // 2)
            else:
                close(half // 2, half)
    gradient(half, nx)
    merge(half, half + 2)
    diffuse(STEPS - 1, 1, quarter + 1)
    merge(half + 2, nx)
    diffuse(STEPS - 1, nx - quarter + 1, nx + 1)
    close(half, nx)
    finish(0, nx)

    for f in range(COEF + 1):
        xdo(f, "wait_send")
        k = f % STEPS
        if f in inputs:
            rdo(f, 0, 1, nx + 1, "wait_send")
        else:
            rdo(f, 0, k + 1, nx + 1 - k, "wait_send")
            rdo(f, 1, 1, k + 1, "wait_send")
            rdo(f, 2, nx + 1 - k, nx + 1, "wait_send")

    @pl.loop(0, nx)
    def _(i):
        @pl.when(is_end)
        def _():
            end_send(i).wait_send()

        @pl.when(is_mid)
        def _():
            peer_send(i).wait_send()
            back_send(i).wait_send()


def shards(sizes, start_conc, target, log_coef, inv_temp, sched_start):
    inverse_temps = lax.dynamic_slice_in_dim(inv_temp, sched_start[0], STEPS)
    rates = 0.16 * jnp.exp(4.0 * (1.0 - inverse_temps))
    nx, ny, nz = log_coef.shape
    f32 = jnp.float32
    field = pltpu.VMEM((nx, ny, nz), f32)
    dma = pltpu.SemaphoreType.DMA
    fields = COEF + 1
    vmem = pl.BlockSpec(memory_space=pltpu.VMEM)
    hbm = pl.BlockSpec(memory_space=pl.ANY)
    return pl.pallas_call(
        functools.partial(body, sizes),
        out_shape=(
            jax.ShapeDtypeStruct(log_coef.shape, f32),
            jax.ShapeDtypeStruct(start_conc.shape, f32),
            jax.ShapeDtypeStruct(start_conc.shape, f32),
        ),
        in_specs=[pl.BlockSpec(memory_space=pltpu.SMEM), hbm, hbm, hbm],
        out_specs=(vmem, vmem, vmem),
        scratch_shapes=[
            pltpu.VMEM((fields, nx + 2, ny + 16, nz), f32),
            pltpu.VMEM((nx + 1, ny, nz), f32),
            field, field, field, field, field, field, field,
            dma((3,)), dma((2 * fields,)), dma((2 * fields,)),
            dma((6 * fields,)), dma((6 * fields,)),
            dma((nx,)), dma((nx,)), dma((nx,)), dma((nx,)),
        ],
        compiler_params=pltpu.CompilerParams(
            collective_id=0, has_side_effects=True, vmem_limit_bytes=60 * 1024 * 1024),
    )(rates, start_conc, target, log_coef)


def solution(mesh):
    placed = (
        P("ens", "gx", "role", None),
        P("ens", "gx", "role", None),
        P("gx", "role", None),
        P(),
        P("ens"),
    )
    return jax.shard_map(
        functools.partial(shards, (mesh.shape["gx"], mesh.shape["role"])),
        mesh=mesh,
        in_specs=placed,
        out_specs=(
            P("gx", "role", None),
            P("ens", "gx", "role", None),
            P("ens", "gx", "role", None),
        ),
        check_vma=False,
    )
```

time: 336 us -> 127 us (0.38)
  other arithmetic: 145 us -> 1.25 us
  Pallas kernels: 0 us -> 118 us
  starting transfers between devices: 90.5 us -> 0 us
  waiting for transfers between devices: 69.9 us -> 0 us
  between operations: 18.8 us -> 1.3 us
    pallas_call x0 -> x1, Pallas kernels: none -> 118 us  [shards(): pl.pallas_call(functools.partial(body, sizes), out_shape=(jax.ShapeDtypeS...]
    ppermute x36 -> x0, starting transfers between devices: 90.5 us -> none  [the longest x18 56.3 us: extended(): lax.ppermute(lax.slice_in_dim(block, 0, width, axis=dim), axis, backward)]
    add x7 -> x0, other arithmetic: 86.6 us -> none  [the longest x1 45 us: shards(): gradient = gradient + rate_list[step] * sensitivity(padded, states[step])]
    psum x1 -> x0, waiting for transfers between devices: 68.5 us -> none  [shards(): coef_grad = coef * lax.psum(gradient, 'ens')]
    concatenate x10 -> x0, other arithmetic: 32.4 us -> none  [extended(): block = jnp.concatenate([low, block, high], axis=dim)]
    broadcast_in_dim x2 -> x0, other arithmetic: 19.7 us -> none  [shards(): return (coef_grad, adjoint[None], current[None])]
    unnamed x130 -> x7, local copies, waits for them, and re-layouts: 4.44 us -> 6.91 us
  transfers between devices with their start and end apart: 37 -> 0, of which waited for: 2 -> 0; matrix products, arithmetic and copies ran while one was open for 22% -> 0% of each run, Pallas kernels for 0% -> 0%
where the time goes in v1:
time: 127 us
  Pallas kernels  118 us (93%)
  local copies, waits for them, and re-layouts  6.91 us (5%)
  between operations  1.3 us (1%)
    pallas_call x1, Pallas kernels, shards(): pl.pallas_call(functools.partial(body, sizes), out_shape=(jax.ShapeDtypeS...  118 us
    unnamed x7, local copies, waits for them, and re-layouts  6.91 us

profile of v1, /device:TPU:6, one launch (start us, length us, event | category | flops | bytes accessed | tf_op | source)
XLA Modules:
  0.0 127.1 jit_solution(13084849016823945724)
XLA Ops:
  1.3 1.3 exponential_multiply_fusion.rates
  2.5 117.7 %shard_map.76 = (f32[16,128,256]{2,1,0:T(8,128)}, f32[1,16,128,256]{3,2,1,0:T(8,128)}, f32[1,16,128,256]{3,2,1,0:T(8,128)}) custom-call(f32[4]{0:T(128)} %exponential_multiply_fusion.rates, f32[1,16,128,256]{3,2,1,0:T(8,128)} %start.1, f32[1,16,128,256]{3,2,1,0:T(8,128)} %target.1, f32[16,128,256]{2,1,0:T(8,128)} %logc.1), custom_call_target="tpu_custom_call" | custom-call | tf_op jit(solution)/shard_map/pallas_call | solution.py:331
  120.2 0.0 copy-start.1
  120.2 3.2 %copy.12 = f32[16,128,256]{2,1,0:T(8,128)} copy(f32[16,128,256]{2,1,0:T(8,128)} %get-tuple-element.6) | data formatting | bytes 4194304
  123.5 0.0 copy-done.1
  123.5 0.0 copy-start
  123.5 1.3 %copy.13 = f32[1,16,128,256]{3,2,1,0:T(8,128)} copy(f32[1,16,128,256]{3,2,1,0:T(8,128)S(1)} %copy-done.1) | data formatting | bytes 4194304
  124.8 1.0 copy-done
  125.8 1.3 %copy.14 = f32[1,16,128,256]{3,2,1,0:T(8,128)} copy(f32[1,16,128,256]{3,2,1,0:T(8,128)S(1)} %copy-done) | data formatting | bytes 4194304
Async XLA Ops:
  120.2 3.3 %copy-start.1 = (f32[1,16,128,256]{3,2,1,0:T(8,128)S(1)}, f32[1,16,128,256]{3,2,1,0:T(8,128)}, u32[]{:S(2)}) copy-start(f32[1,16,128,256]{3,2,1,0:T(8,128)} %get-tuple-element.7) | copy-start | bytes 6291460
  123.5 2.3 %copy-start = (f32[1,16,128,256]{3,2,1,0:T(8,128)S(1)}, f32[1,16,128,256]{3,2,1,0:T(8,128)}, u32[]{:S(2)}) copy-start(f32[1,16,128,256]{3,2,1,0:T(8,128)} %get-tuple-element.8) | copy-start | bytes 6291460

commit v2 on v1

--- a/solution.py
+++ b/solution.py
@@ -14,7 +14,7 @@
 
 def body(
     sizes, rates, start, target, logc, grad_out, adj_out, conc_out,
-    F, wx, wyp, wym, wz, D, G, E, M,
+    F, wx, wyp, wym, wz, D, G, E, M, FX, FY,
     load_sem, xs, xr, rs, rr, sa, sb, re, rm,
 ):
     ngx, nrole = sizes
@@ -152,10 +152,11 @@
                 wp, wm = wyp[p - 1, rows, :], wym[p - 1, rows, :]
                 wr, diag = wz[p - 1, rows, :], D[p - 1, rows, :]
                 for n, (f, rate) in enumerate(pairs):
-                    v = F[f, p, here, :]
+                    wide = F[f, p, pl.ds(y - 8, ROWS + 16), :]
+                    v = wide[8:8 + ROWS]
                     acc = w0 * F[f, p - 1, here, :] + w1 * F[f, p + 1, here, :]
-                    acc = acc + wp * F[f, p, pl.ds(y + 1, ROWS), :]
-                    acc = acc + wm * F[f, p, pl.ds(y - 1, ROWS), :]
+                    acc = acc + wp * wide[9:9 + ROWS]
+                    acc = acc + wm * wide[7:7 + ROWS]
                     acc = acc + wr * pltpu.roll(v, nz - 1, 1) + pltpu.roll(wr * v, 1, 1)
                     new = v + rate * (acc - diag * v)
                     if k < STEPS - 1:
@@ -165,24 +166,43 @@
                     else:
                         adj_out[0, p - 1, rows, :] = new
 
-    def sens(p):
+    def face_x(p):
         for y in chunks:
             here = pl.ds(y, ROWS)
-            up, down = pl.ds(y + 1, ROWS), pl.ds(y - 1, ROWS)
-            result = None
+            total_x = 0.0
+            for s in range(STEPS):
+                cf, af = s, STEPS + (STEPS - 1 - s)
+                da = F[af, p, here, :] - F[af, p + 1, here, :]
+                dc = F[cf, p, here, :] - F[cf, p + 1, here, :]
+                total_x = total_x + rates[s] * (da * dc)
+            FX[p, pl.ds(y - 8, ROWS), :] = total_x
+
+    def sens(p):
+        edge_y = 0.0
+        for s in range(STEPS):
+            cf, af = s, STEPS + (STEPS - 1 - s)
+            da = F[af, p, pl.ds(0, 8), :] - F[af, p, pl.ds(1, 8), :]
+            dc = F[cf, p, pl.ds(0, 8), :] - F[cf, p, pl.ds(1, 8), :]
+            edge_y = edge_y + rates[s] * (da * dc)
+        FY[pl.ds(0, 8), :] = edge_y
+        for y in chunks:
+            here, up = pl.ds(y, ROWS), pl.ds(y + 1, ROWS)
+            rows = pl.ds(y - 8, ROWS)
+            tx, ty, tz, t0 = 0.0, 0.0, 0.0, 0.0
             for s in range(STEPS):
                 cf, af = s, STEPS + (STEPS - 1 - s)
                 c, a = F[cf, p, here, :], F[af, p, here, :]
-                acc = (a - F[af, p - 1, here, :]) * (c - F[cf, p - 1, here, :])
-                acc = acc + (a - F[af, p + 1, here, :]) * (c - F[cf, p + 1, here, :])
-                acc = acc + (a - F[af, p, up, :]) * (c - F[cf, p, up, :])
-                acc = acc + (a - F[af, p, down, :]) * (c - F[cf, p, down, :])
-                face = (a - jnp.where(last, 0.0, pltpu.roll(a, nz - 1, 1))) * (
-                    c - jnp.where(last, 0.0, pltpu.roll(c, nz - 1, 1)))
-                acc = acc + face + jnp.where(first, a * c, pltpu.roll(face, 1, 1))
-                term = (-0.5 * rates[s]) * acc
-                result = term if result is None else result + term
-            G[p - 1, pl.ds(y - 8, ROWS), :] = result
+                tx = tx + rates[s] * ((a - F[af, p + 1, here, :]) * (c - F[cf, p + 1, here, :]))
+                ty = ty + rates[s] * ((a - F[af, p, up, :]) * (c - F[cf, p, up, :]))
+                da = a - jnp.where(last, 0.0, pltpu.roll(a, nz - 1, 1))
+                dc = c - jnp.where(last, 0.0, pltpu.roll(c, nz - 1, 1))
+                tz = tz + rates[s] * (da * dc)
+                t0 = t0 + rates[s] * (a[:, :128] * c[:, :128])
+            FX[p, rows, :] = tx
+            FY[here, :] = ty
+            low_z = jnp.where(first, jnp.concatenate([t0] * (nz // 128), axis=1), pltpu.roll(tz, 1, 1))
+            low_y = FY[pl.ds(y - 1, ROWS), :]
+            G[p - 1, rows, :] = -0.5 * ((tx + FX[p - 1, rows, :]) + (ty + low_y) + (tz + low_z))
 
     def ens_copy(src, dst, send, recv, to):
         return pltpu.make_async_remote_copy(
@@ -214,26 +234,28 @@
             def _():
                 end_send(i).start()
 
+    def merge_one(i):
+        q = plane(i)
+        end_send(i).wait_recv()
+        E[q] = E[q] + G[q]
+        peer_send(i).start()
+
+    def close_one(i):
+        q = plane(i)
+        peer_send(i).wait_recv()
+        G[q] = E[q] + M[q]
+        back_send(i).start()
+        grad_out[q] = 2.0 * F[COEF, q + 1, main, :] * G[q]
+
     def merge(lo, hi):
         @pl.when(is_mid)
         def _():
-            @pl.loop(lo, hi)
-            def _(i):
-                q = plane(i)
-                end_send(i).wait_recv()
-                E[q] = E[q] + G[q]
-                peer_send(i).start()
+            pl.loop(lo, hi)(merge_one)
 
     def close(lo, hi):
         @pl.when(is_mid)
         def _():
-            @pl.loop(lo, hi)
-            def _(i):
-                q = plane(i)
-                peer_send(i).wait_recv()
-                G[q] = E[q] + M[q]
-                back_send(i).start()
-                grad_out[q] = 2.0 * F[COEF, q + 1, main, :] * G[q]
+            pl.loop(lo, hi)(close_one)
 
     def finish(lo, hi):
         @pl.when(is_end)
@@ -248,52 +270,76 @@
     loads[2].wait()
     for f in (0, STEPS):
         rdo(f, 0, 1, nx + 1, "wait_recv")
-    for k in range(STEPS - 1):
+    half = nx // 2
+
+    def inner(k):
         lo, hi = k + 2, nx - k
+        if k > 0:
+            for f in (k, STEPS + k):
+                rdo(f, 0, lo - 1, hi + 1, "wait_recv")
         diffuse(k, lo, hi)
         for f in (k + 1, STEPS + k + 1):
             rdo(f, 0, lo, hi, "start")
-        if k == 0:
-            xdo(COEF, "wait_recv")
-            for p in (0, nx + 1):
-                F[COEF, p, main, :] = 0.5 * jnp.exp(F[COEF, p, main, :])
-            wx_plane(0)
-            wx_plane(nx)
-            diag_plane(1)
-            diag_plane(nx)
-        for f in (k + 1, STEPS + k + 1):
-            rdo(f, 0, lo, hi, "wait_recv")
-    gradient(0, nx // 2)
-
-    half = nx // 2
-    third = half // 3
-    for k in range(STEPS):
+
+    def arrive(k):
         for f in (k, STEPS + k):
             xdo(f, "wait_recv")
             if k > 0:
                 rdo(f, 1, 1, k + 1, "wait_recv")
                 rdo(f, 2, nx + 1 - k, nx + 1, "wait_recv")
-        if k < STEPS - 1:
-            diffuse(k, 1, k + 2)
-            diffuse(k, nx - k, nx + 1)
-            for f in (k + 1, STEPS + k + 1):
-                xdo(f, "start")
-                rdo(f, 1, 1, k + 2, "start")
-                rdo(f, 2, nx - k, nx + 1, "start")
-            if k == 0:
-                merge(0, half // 2)
-                diffuse(STEPS - 1, quarter + 1, nx - quarter + 1)
-            elif k == 1:
-                merge(half // 2, half)
-                close(0, half // 2)
-            else:
-                close(half // 2, half)
+
+    def outer(k):
+        arrive(k)
+        for lo, hi in ((1, 2), (nx, nx + 1)):
+            diffuse(k, lo, hi)
+        for f in (k + 1, STEPS + k + 1):
+            xdo(f, "start")
+        if k > 0:
+            diffuse(k, 2, k + 2)
+            diffuse(k, nx - k, nx)
+        for f in (k + 1, STEPS + k + 1):
+            rdo(f, 1, 1, k + 2, "start")
+            rdo(f, 2, nx - k, nx + 1, "start")
+
+    inner(0)
+    xdo(COEF, "wait_recv")
+    for p in (0, nx + 1):
+        F[COEF, p, main, :] = 0.5 * jnp.exp(F[COEF, p, main, :])
+    wx_plane(0)
+    wx_plane(nx)
+    diag_plane(1)
+    diag_plane(nx)
+    inner(1)
+    outer(0)
+    inner(2)
+    for f in (STEPS - 1, COEF - 1):
+        rdo(f, 0, STEPS, nx - STEPS + 2, "wait_recv")
+    face_x(quarter)
+    gradient(0, half)
+    outer(1)
+    merge(0, 2)
+    diffuse(STEPS - 1, quarter + 1, nx - quarter + 1)
+    merge(2, 4)
+    close(0, 2)
+    outer(2)
+    merge(4, half)
+    close(2, 5)
+    arrive(STEPS - 1)
+    face_x(0)
     gradient(half, nx)
-    merge(half, half + 2)
+    close(5, half)
     diffuse(STEPS - 1, 1, quarter + 1)
-    merge(half + 2, nx)
+    merge(half, half + 1)
     diffuse(STEPS - 1, nx - quarter + 1, nx + 1)
-    close(half, nx)
+    merge(half + 1, half + 2)
+
+    @pl.when(is_mid)
+    def _():
+        @pl.loop(half + 2, nx)
+        def _(i):
+            merge_one(i)
+            close_one(i - 2)
+    close(nx - 2, nx)
     finish(0, nx)
 
     for f in range(COEF + 1):
@@ -341,6 +387,7 @@
             pltpu.VMEM((fields, nx + 2, ny + 16, nz), f32),
             pltpu.VMEM((nx + 1, ny, nz), f32),
             field, field, field, field, field, field, field,
+            pltpu.VMEM((nx + 1, ny, nz), f32), pltpu.VMEM((ny + 16, nz), f32),
             dma((3,)), dma((2 * fields,)), dma((2 * fields,)),
             dma((6 * fields,)), dma((6 * fields,)),
             dma((nx,)), dma((nx,)), dma((nx,)), dma((nx,)),

time: 127 us -> 107 us (0.84)
  Pallas kernels: 118 us -> 97.6 us
    pallas_call x1, Pallas kernels: 118 us -> 97.6 us  [shards(): pl.pallas_call(functools.partial(body, sizes), out_shape=(jax.ShapeDtypeS...]
where the time goes in v2:
time: 107 us
  Pallas kernels  97.6 us (91%)
  local copies, waits for them, and re-layouts  6.91 us (6%)
  between operations  1.3 us (1%)
  other arithmetic  1.25 us (1%)
    pallas_call x1, Pallas kernels, shards(): pl.pallas_call(functools.partial(body, sizes), out_shape=(jax.ShapeDtypeS...  97.6 us
    unnamed x7, local copies, waits for them, and re-layouts  6.91 us

profile of v2, /device:TPU:6, one launch (start us, length us, event | category | flops | bytes accessed | tf_op | source)
XLA Modules:
  0.0 107.0 jit_solution(15644551781034594598)
XLA Ops:
  1.3 1.3 %exponential_multiply_fusion.rates = f32[4]{0:T(128)} fusion(f32[64]{0:T(128)} %param.8, s32[]{:T(128)S(6)} %select_n.3), kind=kLoop, calls=%fused_computation | loop fusion | flops 12 | bytes 36 | tf_op jit(solution)/shard_map/mul | solution.py:369
  2.5 97.6 %shard_map.76 = (f32[16,128,256]{2,1,0:T(8,128)}, f32[1,16,128,256]{3,2,1,0:T(8,128)}, f32[1,16,128,256]{3,2,1,0:T(8,128)}) custom-call(f32[4]{0:T(128)} %exponential_multiply_fusion.rates, f32[1,16,128,256]{3,2,1,0:T(8,128)} %start.1, f32[1,16,128,256]{3,2,1,0:T(8,128)} %target.1, f32[16,128,256]{2,1,0:T(8,128)} %logc.1), custom_call_target="tpu_custom_call" | custom-call | tf_op jit(solution)/shard_map/pallas_call | solution.py:377
  100.1 0.0 copy-start.1
  100.1 3.2 %copy.12 = f32[16,128,256]{2,1,0:T(8,128)} copy(f32[16,128,256]{2,1,0:T(8,128)} %get-tuple-element.6) | data formatting | bytes 4194304
  103.4 0.0 copy-done.1
  103.4 0.0 copy-start
  103.4 1.3 %copy.13 = f32[1,16,128,256]{3,2,1,0:T(8,128)} copy(f32[1,16,128,256]{3,2,1,0:T(8,128)S(1)} %copy-done.1) | data formatting | bytes 4194304
  104.7 1.0 copy-done
  105.7 1.3 %copy.14 = f32[1,16,128,256]{3,2,1,0:T(8,128)} copy(f32[1,16,128,256]{3,2,1,0:T(8,128)S(1)} %copy-done) | data formatting | bytes 4194304
Async XLA Ops:
  100.1 3.3 %copy-start.1 = (f32[1,16,128,256]{3,2,1,0:T(8,128)S(1)}, f32[1,16,128,256]{3,2,1,0:T(8,128)}, u32[]{:S(2)}) copy-start(f32[1,16,128,256]{3,2,1,0:T(8,128)} %get-tuple-element.7) | copy-start | bytes 6291460
  103.4 2.3 %copy-start = (f32[1,16,128,256]{3,2,1,0:T(8,128)S(1)}, f32[1,16,128,256]{3,2,1,0:T(8,128)}, u32[]{:S(2)}) copy-start(f32[1,16,128,256]{3,2,1,0:T(8,128)} %get-tuple-element.8) | copy-start | bytes 6291460

commit v3 on v2

--- a/solution.py
+++ b/solution.py
@@ -8,6 +8,7 @@
 
 STEPS = 4
 COEF = 2 * STEPS
+PARTS = 2 * STEPS - 1
 ROWS = 32
 FAR = -1e30
 
@@ -51,7 +52,7 @@
             src = inputs[f].at[:, pl.ds(row, 8)]
         else:
             src = F.at[f, planes, pl.ds(row + 8, 8)]
-        sem = (2 * f + d) * 3 + part
+        sem = (2 * f + d) * PARTS + part
         return pltpu.make_async_remote_copy(
             src, F.at[f, planes, pl.ds(0 if d else ny + 8, 8)], rs.at[sem], rr.at[sem],
             device_id={"role": role + (1 if d else -1)}, device_id_type=pl.DeviceIdType.MESH)
@@ -208,10 +209,12 @@
         return pltpu.make_async_remote_copy(
             src, dst, send, recv, device_id={"ens": to}, device_id_type=pl.DeviceIdType.MESH)
 
-    quarter = nx // 4
+    quarter, half = STEPS, nx - 2 * STEPS
 
     def plane(i):
-        return lax.rem(i + quarter, nx)
+        outside, side, ring = lax.div(i, half), lax.rem(i, 2), lax.div(i, 2) - half // 2
+        pair = quarter - 1 - ring + side * (half + 1 + 2 * ring)
+        return (1 - outside) * (i + quarter) + outside * pair
 
     def end_send(i):
         q = plane(i)
@@ -270,8 +273,6 @@
     loads[2].wait()
     for f in (0, STEPS):
         rdo(f, 0, 1, nx + 1, "wait_recv")
-    half = nx // 2
-
     def inner(k):
         lo, hi = k + 2, nx - k
         if k > 0:
@@ -281,25 +282,30 @@
         for f in (k + 1, STEPS + k + 1):
             rdo(f, 0, lo, hi, "start")
 
+    def single(level, q, do):
+        for f in (level, STEPS + level):
+            rdo(f, 2 * q - 1, q, q + 1, do)
+            rdo(f, 2 * q, nx + 1 - q, nx + 2 - q, do)
+
     def arrive(k):
         for f in (k, STEPS + k):
             xdo(f, "wait_recv")
+        for level in range(max(k, 1), STEPS):
             if k > 0:
-                rdo(f, 1, 1, k + 1, "wait_recv")
-                rdo(f, 2, nx + 1 - k, nx + 1, "wait_recv")
-
-    def outer(k):
-        arrive(k)
-        for lo, hi in ((1, 2), (nx, nx + 1)):
-            diffuse(k, lo, hi)
-        for f in (k + 1, STEPS + k + 1):
-            xdo(f, "start")
-        if k > 0:
-            diffuse(k, 2, k + 2)
-            diffuse(k, nx - k, nx)
-        for f in (k + 1, STEPS + k + 1):
-            rdo(f, 1, 1, k + 2, "start")
-            rdo(f, 2, nx - k, nx + 1, "start")
+                single(level, level - k + 1, "wait_recv")
+
+    def wave(k, j):
+        q = j - k + 1
+        diffuse(j, q, q + 1)
+        diffuse(j, nx + 1 - q, nx + 2 - q)
+        if j == k:
+            for f in (k + 1, STEPS + k + 1):
+                xdo(f, "start")
+        single(j + 1, q, "start")
+
+    def ring(k):
+        face_x(quarter - k - 1)
+        gradient(half + 2 * k, half + 2 * k + 2)
 
     inner(0)
     xdo(COEF, "wait_recv")
@@ -310,28 +316,37 @@
     diag_plane(1)
     diag_plane(nx)
     inner(1)
-    outer(0)
+    arrive(0)
+    wave(0, 0)
     inner(2)
     for f in (STEPS - 1, COEF - 1):
         rdo(f, 0, STEPS, nx - STEPS + 2, "wait_recv")
     face_x(quarter)
     gradient(0, half)
-    outer(1)
-    merge(0, 2)
+    wave(0, 1)
+    wave(0, 2)
+    ring(0)
+    arrive(1)
+    wave(1, 1)
+    wave(1, 2)
+    ring(1)
+    merge(0, 3)
     diffuse(STEPS - 1, quarter + 1, nx - quarter + 1)
-    merge(2, 4)
+    merge(3, 5)
     close(0, 2)
-    outer(2)
-    merge(4, half)
+    arrive(2)
+    wave(2, 2)
+    ring(2)
+    merge(5, half)
     close(2, 5)
-    arrive(STEPS - 1)
-    face_x(0)
-    gradient(half, nx)
-    close(5, half)
+    arrive(3)
+    ring(3)
+    merge(half, half + 1)
+    close(5, 7)
     diffuse(STEPS - 1, 1, quarter + 1)
-    merge(half, half + 1)
+    merge(half + 1, half + 2)
+    close(7, half)
     diffuse(STEPS - 1, nx - quarter + 1, nx + 1)
-    merge(half + 1, half + 2)
 
     @pl.when(is_mid)
     def _():
@@ -349,8 +364,9 @@
             rdo(f, 0, 1, nx + 1, "wait_send")
         else:
             rdo(f, 0, k + 1, nx + 1 - k, "wait_send")
-            rdo(f, 1, 1, k + 1, "wait_send")
-            rdo(f, 2, nx + 1 - k, nx + 1, "wait_send")
+            for q in range(1, k + 1):
+                rdo(f, 2 * q - 1, q, q + 1, "wait_send")
+                rdo(f, 2 * q, nx + 1 - q, nx + 2 - q, "wait_send")
 
     @pl.loop(0, nx)
     def _(i):
@@ -389,7 +405,7 @@
             field, field, field, field, field, field, field,
             pltpu.VMEM((nx + 1, ny, nz), f32), pltpu.VMEM((ny + 16, nz), f32),
             dma((3,)), dma((2 * fields,)), dma((2 * fields,)),
-            dma((6 * fields,)), dma((6 * fields,)),
+            dma((2 * PARTS * fields,)), dma((2 * PARTS * fields,)),
             dma((nx,)), dma((nx,)), dma((nx,)), dma((nx,)),
         ],
         compiler_params=pltpu.CompilerParams(

time: 107 us -> 109 us (1.019); the launches traced: 107 us -> 108 us
  no operation moved by 1% of the time
where the time goes in v3:
time: 109 us; the launch traced here: 108 us
  Pallas kernels  98.2 us (90%)
  local copies, waits for them, and re-layouts  6.91 us (6%)
  between operations  1.3 us (1%)
  other arithmetic  1.25 us (1%)
    pallas_call x1, Pallas kernels, shards(): pl.pallas_call(functools.partial(body, sizes), out_shape=(jax.ShapeDtypeS...  98.2 us
    unnamed x7, local copies, waits for them, and re-layouts  6.91 us

profile of v3, /device:TPU:6, one launch (start us, length us, event | category | flops | bytes accessed | tf_op | source)
XLA Modules:
  0.0 107.7 jit_solution(2268416553098177886)
XLA Ops:
  1.3 1.3 %exponential_multiply_fusion.rates = f32[4]{0:T(128)} fusion(f32[64]{0:T(128)} %param.8, s32[]{:T(128)S(6)} %select_n.3), kind=kLoop, calls=%fused_computation | loop fusion | flops 12 | bytes 36 | tf_op jit(solution)/shard_map/mul | solution.py:385
  2.5 98.2 %shard_map.76 = (f32[16,128,256]{2,1,0:T(8,128)}, f32[1,16,128,256]{3,2,1,0:T(8,128)}, f32[1,16,128,256]{3,2,1,0:T(8,128)}) custom-call(f32[4]{0:T(128)} %exponential_multiply_fusion.rates, f32[1,16,128,256]{3,2,1,0:T(8,128)} %start.1, f32[1,16,128,256]{3,2,1,0:T(8,128)} %target.1, f32[16,128,256]{2,1,0:T(8,128)} %logc.1), custom_call_target="tpu_custom_call" | custom-call | tf_op jit(solution)/shard_map/pallas_call | solution.py:393
  100.8 0.0 copy-start.1
  100.8 3.2 %copy.12 = f32[16,128,256]{2,1,0:T(8,128)} copy(f32[16,128,256]{2,1,0:T(8,128)} %get-tuple-element.6) | data formatting | bytes 4194304
  104.0 0.0 copy-done.1
  104.0 0.0 copy-start
  104.0 1.3 %copy.13 = f32[1,16,128,256]{3,2,1,0:T(8,128)} copy(f32[1,16,128,256]{3,2,1,0:T(8,128)S(1)} %copy-done.1) | data formatting | bytes 4194304
  105.3 1.0 copy-done
  106.4 1.3 %copy.14 = f32[1,16,128,256]{3,2,1,0:T(8,128)} copy(f32[1,16,128,256]{3,2,1,0:T(8,128)S(1)} %copy-done) | data formatting | bytes 4194304
Async XLA Ops:
  100.8 3.3 %copy-start.1 = (f32[1,16,128,256]{3,2,1,0:T(8,128)S(1)}, f32[1,16,128,256]{3,2,1,0:T(8,128)}, u32[]{:S(2)}) copy-start(f32[1,16,128,256]{3,2,1,0:T(8,128)} %get-tuple-element.7) | copy-start | bytes 6291460
  104.0 2.3 %copy-start = (f32[1,16,128,256]{3,2,1,0:T(8,128)S(1)}, f32[1,16,128,256]{3,2,1,0:T(8,128)}, u32[]{:S(2)}) copy-start(f32[1,16,128,256]{3,2,1,0:T(8,128)} %get-tuple-element.8) | copy-start | bytes 6291460

commit v4 on v3

--- a/solution.py
+++ b/solution.py
@@ -323,26 +323,35 @@
         rdo(f, 0, STEPS, nx - STEPS + 2, "wait_recv")
     face_x(quarter)
     gradient(0, half)
+    merge(0, 1)
     wave(0, 1)
+    merge(1, 2)
     wave(0, 2)
     ring(0)
+    merge(2, 3)
     arrive(1)
     wave(1, 1)
+    merge(3, 4)
+    close(0, 1)
     wave(1, 2)
     ring(1)
-    merge(0, 3)
-    diffuse(STEPS - 1, quarter + 1, nx - quarter + 1)
-    merge(3, 5)
-    close(0, 2)
+    merge(4, 5)
+    close(1, 2)
+    diffuse(STEPS - 1, quarter + 1, half + 1)
+    merge(5, 6)
+    close(2, 3)
     arrive(2)
     wave(2, 2)
     ring(2)
-    merge(5, half)
-    close(2, 5)
+    merge(6, 7)
+    close(3, 5)
+    diffuse(STEPS - 1, half + 1, nx - quarter + 1)
+    merge(7, half)
+    close(5, 6)
     arrive(3)
     ring(3)
     merge(half, half + 1)
-    close(5, 7)
+    close(6, 7)
     diffuse(STEPS - 1, 1, quarter + 1)
     merge(half + 1, half + 2)
     close(7, half)

time: 109 us -> 109 us (level)
  no operation moved by 1% of the time
where the time goes in v4:
time: 109 us
  Pallas kernels  99.1 us (91%)
  local copies, waits for them, and re-layouts  6.91 us (6%)
  between operations  1.3 us (1%)
  other arithmetic  1.25 us (1%)
    pallas_call x1, Pallas kernels, shards(): pl.pallas_call(functools.partial(body, sizes), out_shape=(jax.ShapeDtypeS...  99.1 us
    unnamed x7, local copies, waits for them, and re-layouts  6.91 us

profile of v4, /device:TPU:6, one launch (start us, length us, event | category | flops | bytes accessed | tf_op | source)
XLA Modules:
  0.0 108.5 jit_solution(2732929524974351249)
XLA Ops:
  1.3 1.3 %exponential_multiply_fusion.rates = f32[4]{0:T(128)} fusion(f32[64]{0:T(128)} %param.8, s32[]{:T(128)S(6)} %select_n.3), kind=kLoop, calls=%fused_computation | loop fusion | flops 12 | bytes 36 | tf_op jit(solution)/shard_map/mul | solution.py:394
  2.5 99.1 %shard_map.76 = (f32[16,128,256]{2,1,0:T(8,128)}, f32[1,16,128,256]{3,2,1,0:T(8,128)}, f32[1,16,128,256]{3,2,1,0:T(8,128)}) custom-call(f32[4]{0:T(128)} %exponential_multiply_fusion.rates, f32[1,16,128,256]{3,2,1,0:T(8,128)} %start.1, f32[1,16,128,256]{3,2,1,0:T(8,128)} %target.1, f32[16,128,256]{2,1,0:T(8,128)} %logc.1), custom_call_target="tpu_custom_call" | custom-call | tf_op jit(solution)/shard_map/pallas_call | solution.py:402
  101.6 0.0 copy-start.1
  101.6 3.2 %copy.12 = f32[16,128,256]{2,1,0:T(8,128)} copy(f32[16,128,256]{2,1,0:T(8,128)} %get-tuple-element.6) | data formatting | bytes 4194304
  104.9 0.0 copy-done.1
  104.9 0.0 copy-start
  104.9 1.3 %copy.13 = f32[1,16,128,256]{3,2,1,0:T(8,128)} copy(f32[1,16,128,256]{3,2,1,0:T(8,128)S(1)} %copy-done.1) | data formatting | bytes 4194304
  106.2 1.0 copy-done
  107.2 1.3 %copy.14 = f32[1,16,128,256]{3,2,1,0:T(8,128)} copy(f32[1,16,128,256]{3,2,1,0:T(8,128)S(1)} %copy-done) | data formatting | bytes 4194304
Async XLA Ops:
  101.6 3.3 %copy-start.1 = (f32[1,16,128,256]{3,2,1,0:T(8,128)S(1)}, f32[1,16,128,256]{3,2,1,0:T(8,128)}, u32[]{:S(2)}) copy-start(f32[1,16,128,256]{3,2,1,0:T(8,128)} %get-tuple-element.7) | copy-start | bytes 6291460
  104.9 2.3 %copy-start = (f32[1,16,128,256]{3,2,1,0:T(8,128)S(1)}, f32[1,16,128,256]{3,2,1,0:T(8,128)}, u32[]{:S(2)}) copy-start(f32[1,16,128,256]{3,2,1,0:T(8,128)} %get-tuple-element.8) | copy-start | bytes 6291460
